TPU v7x, 512 devices: a whole 4x8x8 slice. The times are simulated.
512 devices in a mesh: ctx: 16 (over x_lo, y), chan: 32 (over z, x_hi, core).
Axes of the slice: x: 4 (x_hi: 2, x_lo: 2; x = x_hi * 2 + x_lo), y: 8, z: 8, core: 2. Of those that a mesh axis runs over, the one named last changes fastest.
Arguments:
- query_proj: bfloat16 [8192, 4096], P('chan', 'ctx'), may hold values from -6 to 6
- key_proj: bfloat16 [8192, 4096], P('chan', 'ctx'), may hold values from -6 to 6
- value_proj: bfloat16 [8192, 4096], P('chan', 'ctx'), may hold values from -6 to 6
- out_cotangent: bfloat16 [8192, 4096], P('chan', 'ctx'), may hold values from -6 to 6
- short_taps: float32 [3, 7, 8192], P(None, None, 'chan'), may hold values from -2 to 2
- filter_in: float32 [33, 64], replicated, may hold values from -1 to 1
- filter_out: float32 [64, 8192], P(None, ('chan', 'ctx')), may hold values from -9 to 9
- decay_rate: float32 [8192], P(('chan', 'ctx')), may hold values from 0.5 to 400
- skip_gain: float32 [8192], P(('chan', 'ctx')), may hold values from -4 to 4
Outputs:
- mixed: bfloat16 [8192, 4096], P('chan', 'ctx')
- query_grad: bfloat16 [8192, 4096], P('chan', 'ctx')
- key_grad: bfloat16 [8192, 4096], P('chan', 'ctx')
- value_grad: bfloat16 [8192, 4096], P('chan', 'ctx')
- taps_grad: float32 [3, 7, 8192], P(None, None, 'chan')
- filter_in_grad: float32 [33, 64], replicated
- filter_out_grad: float32 [64, 8192], P(None, ('chan', 'ctx'))
- skip_grad: float32 [8192], P(('chan', 'ctx'))
All inputs are finite; a program needn't handle non-finite values.
Results may differ from a plain program's by a relative error of at most 0.0057.
Values may be sent and summed in bfloat16 or wider, within the bound.
A program may use at most 64 MiB of HBM per device.

v0:
```python
import math

import jax
import jax.numpy as jnp
from jax import lax
from jax.sharding import PartitionSpec as P

D = 8192


HIGH = lax.Precision.HIGHEST


def shifted(x, axis, by):
    devices = lax.axis_size(axis)
    pairs = [(i, i + by) for i in range(devices) if 0 <= i + by < devices]
    return lax.ppermute(x, axis, pairs)


def position_features(length, emb):
    bands = (emb - 1) // 2
    places = jnp.arange(length, dtype=jnp.int32)
    freqs = jnp.arange(1, bands + 1, dtype=jnp.int32)
    phase = (freqs[:, None] * places[None, :] % length).astype(jnp.float32) * (
        2.0 * math.pi / length
    )
    ramp = places.astype(jnp.float32)[None, :] / length
    return jnp.concatenate([ramp, jnp.cos(phase), jnp.sin(phase)], axis=0)


def split_length(total):
    best = 2
    for factor in range(2, math.isqrt(total) + 1, 2):
        if total % factor == 0:
            best = factor
    return best


def angle_table(rows, cols, period):
    left = jnp.arange(rows, dtype=jnp.int32)[:, None]
    right = jnp.arange(cols, dtype=jnp.int32)[None, :]
    phase = (left * right % period).astype(jnp.float32) * (2.0 * math.pi / period)
    return (jnp.cos(phase), jnp.sin(phase))


def make_plan(total):
    first = split_length(total)
    second = total // first
    cos_first, sin_first = angle_table(first, first, first)
    cos_second, sin_second = angle_table(second, second, second)
    twist_cos, twist_sin = angle_table(first, second, total)
    return (first, second, cos_first, sin_first, cos_second, sin_second, twist_cos, twist_sin)


def spectrum(signal, plan):
    first, second, cos_first, sin_first, cos_second, sin_second, twist_cos, twist_sin = plan
    half = first // 2
    channels = signal.shape[0]
    folded = signal.reshape(channels, half, second)
    real_a = jnp.einsum("kn,cnm->ckm", cos_first[:, :half], folded, precision=HIGH)
    imag_a = -jnp.einsum("kn,cnm->ckm", sin_first[:, :half], folded, precision=HIGH)
    real_b = real_a * twist_cos + imag_a * twist_sin
    imag_b = imag_a * twist_cos - real_a * twist_sin
    real_x = jnp.einsum("ckn,nm->ckm", real_b, cos_second, precision=HIGH) + jnp.einsum(
        "ckn,nm->ckm", imag_b, sin_second, precision=HIGH
    )
    imag_x = jnp.einsum("ckn,nm->ckm", imag_b, cos_second, precision=HIGH) - jnp.einsum(
        "ckn,nm->ckm", real_b, sin_second, precision=HIGH
    )
    return (real_x, imag_x)


def signal_of(real_x, imag_x, plan):
    first, second, cos_first, sin_first, cos_second, sin_second, twist_cos, twist_sin = plan
    half = first // 2
    channels = real_x.shape[0]
    real_c = jnp.einsum("ckn,nm->ckm", real_x, cos_second, precision=HIGH) - jnp.einsum(
        "ckn,nm->ckm", imag_x, sin_second, precision=HIGH
    )
    imag_c = jnp.einsum("ckn,nm->ckm", imag_x, cos_second, precision=HIGH) + jnp.einsum(
        "ckn,nm->ckm", real_x, sin_second, precision=HIGH
    )
    real_d = real_c * twist_cos - imag_c * twist_sin
    imag_d = imag_c * twist_cos + real_c * twist_sin
    result = jnp.einsum("nk,ckm->cnm", cos_first[:half, :], real_d, precision=HIGH) - jnp.einsum(
        "nk,ckm->cnm", sin_first[:half, :], imag_d, precision=HIGH
    )
    return result.reshape(channels, half * second) / (first * second)


def per_device(
    query_proj,
    key_proj,
    value_proj,
    out_cotangent,
    short_taps,
    filter_in,
    filter_out,
    decay_rate,
    skip_gain,
):
    reach = short_taps.shape[1] - 1
    rows = query_proj.shape[1]
    seq_total = rows * lax.axis_size("ctx")
    scale = 1.0 / math.sqrt(seq_total)
    stacked = jnp.stack([query_proj, key_proj, value_proj])
    tails = shifted(stacked[:, :, rows - reach :], "ctx", 1)
    padded = jnp.concatenate([tails, stacked], axis=2).astype(jnp.float32)
    shorts = jnp.zeros(stacked.shape, jnp.float32)
    for offset in range(reach + 1):
        shorts = (
            shorts
            + short_taps[:, offset, :, None] * padded[:, :, reach - offset : reach - offset + rows]
        )
    q_short, k_short, v_short = (shorts[0], shorts[1], shorts[2])
    cotan = out_cotangent.astype(jnp.float32)
    mixer_in = (k_short * v_short).astype(jnp.bfloat16)
    grad_in = (cotan * q_short).astype(jnp.bfloat16)
    mixer_cols = lax.all_to_all(mixer_in, "ctx", split_axis=0, concat_axis=1, tiled=True)
    length = mixer_cols.shape[1]
    features = position_features(length, filter_in.shape[0])
    pre = jnp.dot(filter_in.T, features, precision=HIGH, preferred_element_type=jnp.float32)
    act = jnp.sin(pre)
    envelope = jnp.exp(-decay_rate[:, None] * features[0:1]) * scale
    raw = jnp.dot(filter_out.T, act, precision=HIGH, preferred_element_type=jnp.float32)
    filt = raw * envelope
    plan = make_plan(2 * length)
    mixer_f = mixer_cols.astype(jnp.float32)
    real_h, imag_h = spectrum(filt, plan)
    real_u, imag_u = spectrum(mixer_f, plan)
    conv = signal_of(real_u * real_h - imag_u * imag_h, real_u * imag_h + imag_u * real_h, plan)
    conv = (conv + skip_gain[:, None] * mixer_f).astype(jnp.bfloat16)
    state = (features, pre, act, envelope, plan, mixer_f, real_h, imag_h, real_u, imag_u)
    conv_cols, state = (conv, state)
    conv_rows = lax.all_to_all(conv_cols, "ctx", split_axis=1, concat_axis=0, tiled=True)
    grad_cols = lax.all_to_all(grad_in, "ctx", split_axis=0, concat_axis=1, tiled=True)
    features, pre, act, envelope, plan, mixer_f, real_h, imag_h, real_u, imag_u = state
    grad_f = grad_cols.astype(jnp.float32)
    real_g, imag_g = spectrum(grad_f, plan)
    back = signal_of(real_g * real_h + imag_g * imag_h, imag_g * real_h - real_g * imag_h, plan)
    back = (back + skip_gain[:, None] * grad_f).astype(jnp.bfloat16)
    filt_grad = signal_of(
        real_g * real_u + imag_g * imag_u, imag_g * real_u - real_g * imag_u, plan
    )
    skip_local = jnp.sum(grad_f * mixer_f, axis=1) * scale
    bent = filt_grad * envelope
    out_local = jnp.einsum("ft,ct->fc", act, bent, precision=HIGH) * scale
    act_grad = jnp.einsum("fc,ct->ft", filter_out, bent, precision=HIGH)
    in_part = jnp.einsum("et,ft->ef", features, act_grad * jnp.cos(pre), precision=HIGH)
    back_cols, out_local, skip_local, in_part = (back, out_local, skip_local, in_part)
    back_rows = lax.all_to_all(back_cols, "ctx", split_axis=1, concat_axis=0, tiled=True)
    conv_f = conv_rows.astype(jnp.float32)
    back_f = back_rows.astype(jnp.float32)
    mixed = (q_short * conv_f).astype(jnp.bfloat16)
    grads = jnp.stack([cotan * conv_f, back_f * v_short, back_f * k_short])
    heads = shifted(grads[:, :, :reach], "ctx", -1)
    extended = jnp.concatenate([grads, heads], axis=2)
    in_grads = jnp.zeros(grads.shape, jnp.float32)
    tap_list = []
    for offset in range(reach + 1):
        in_grads = (
            in_grads + short_taps[:, offset, :, None] * extended[:, :, offset : offset + rows]
        )
        tap_list.append(
            jnp.sum(grads * padded[:, :, reach - offset : reach - offset + rows], axis=2) * scale
        )
    tap_local = jnp.stack(tap_list, axis=1)
    in_grads = in_grads.astype(jnp.bfloat16)
    in_scale = scale / math.sqrt(D)
    tap_total = lax.psum(tap_local, "ctx")
    in_total = lax.psum(in_part, ("ctx", "chan"))
    return (
        mixed,
        in_grads[0],
        in_grads[1],
        in_grads[2],
        tap_total,
        in_total * in_scale,
        out_local,
        skip_local,
    )


def solution(mesh):
    return jax.shard_map(
        per_device,
        mesh=mesh,
        in_specs=(
            P("chan", "ctx"),
            P("chan", "ctx"),
            P("chan", "ctx"),
            P("chan", "ctx"),
            P(None, None, "chan"),
            P(),
            P(None, ("chan", "ctx")),
            P(("chan", "ctx")),
            P(("chan", "ctx")),
        ),
        out_specs=(
            P("chan", "ctx"),
            P("chan", "ctx"),
            P("chan", "ctx"),
            P("chan", "ctx"),
            P(None, None, "chan"),
            P(),
            P(None, ("chan", "ctx")),
            P(("chan", "ctx")),
        ),
        check_vma=False,
    )
```

profile of v0, /device:TPU:2, one launch (start us, length us, event | category | flops | bytes accessed | tf_op | source)
XLA Modules:
  0.0 304.1 jit_solution(1840900404118238585)
XLA Ops:
  0.7 1.0 pad_maximum_fusion.5
  1.7 3.5 %collective-permute-start = (bf16[3,256,6]{2,1,0:T(8,128)(2,1)S(1)}, bf16[3,256,6]{2,1,0:T(8,128)(2,1)S(1)}, u32[]{:S(2)}, u32[]{:S(2)}) collective-permute-start(bf16[3,256,6]{2,1,0:T(8,128)(2,1)S(1)} %pad_maximum_fusion.5), channel_id=1, source_target_pairs={{0,32},{32,64},{64,96},{96,128},{128,160},{160,192},{192,224},{224... | collective-permute-start | bytes 27656 | tf_op jit(solution)/shard_map/ppermute | solution.py:17
  5.7 1.1 fusion.79
  6.9 5.7 %fusion.259 = (f32[4096,64]{0,1:T(8,128)S(1)}, f32[4096,64]{0,1:T(8,128)}) fusion(f32[33,64]{1,0:T(8,128)S(1)} %copy-done, f32[16,4096]{1,0:T(8,128)S(1)} %get-tuple-element.63, f32[16,4096]{1,0:T(8,128)S(1)} %get-tuple-element.62, f32[1,4096]{1,0:T(1,128)S(1)} %convert_multiply_fusion.6), kind=kOutput, calls=%fused_computation.341 | convolution fusion | flops 104079360 | bytes 2646272 | tf_op jit(solution)/shard_map/dot_general | solution.py:122
  14.6 0.8 fusion.68
  15.4 1.6 fusion.69
  17.1 1.6 convolution_add_fusion.4
  19.1 2.1 multiply_add_fusion
  21.3 0.9 copy-done.1
  22.8 7.7 %all-to-all-start = ((bf16[16,16,256]{2,1,0:T(8,128)(2,1)}), bf16[16,16,256]{2,1,0:T(8,128)(2,1)S(1)}, u32[]{:S(2)}, u32[]{:S(2)}) async-start(bf16[16,16,256]{2,1,0:T(8,128)(2,1)} %bitcast.202), calls=%async_computation | async-start | bytes 262144 | tf_op jit(solution)/shard_map/all_to_all | solution.py:119
  30.5 2.7 convolution_subtract_fusion.4
  33.2 1.6 fusion.43
  34.9 3.2 %all-to-all-done = bf16[16,16,256]{2,1,0:T(8,128)(2,1)S(1)} async-done(((bf16[16,16,256]{2,1,0:T(8,128)(2,1)}), bf16[16,16,256]{2,1,0:T(8,128)(2,1)S(1)}, u32[]{:S(2)}, u32[]{:S(2)}) %all-to-all-start) | async-done | bytes 131104 | tf_op jit(solution)/shard_map/all_to_all | solution.py:119
  38.1 5.3 %all-to-all-start.2 = ((bf16[16,16,256]{2,1,0:T(8,128)(2,1)}), bf16[16,16,256]{2,1,0:T(8,128)(2,1)}, u32[]{:S(2)}, u32[]{:S(2)}) async-start(bf16[16,16,256]{2,1,0:T(8,128)(2,1)} %bitcast.22), calls=%async_computation.2 | async-start | bytes 262144 | tf_op jit(solution)/shard_map/all_to_all | solution.py:136
  44.5 1.3 fusion.3
  45.9 5.0 %all-to-all-done.2 = bf16[16,16,256]{2,1,0:T(8,128)(2,1)} async-done(((bf16[16,16,256]{2,1,0:T(8,128)(2,1)}), bf16[16,16,256]{2,1,0:T(8,128)(2,1)}, u32[]{:S(2)}, u32[]{:S(2)}) %all-to-all-start.2) | async-done | bytes 131104 | tf_op jit(solution)/shard_map/all_to_all | solution.py:136
  50.9 1.6 copy.48
  52.5 1.6 reshape.205
  54.1 1.3 fusion.1
  55.4 1.3 convolution_bitcast_fusion.1
  56.7 0.8 fusion.67
  59.2 0.8 fusion.71
  60.0 0.8 convolution_subtract_fusion.5
  60.9 0.8 convolution_add_fusion.2
  61.7 0.8 convolution_add_fusion.5
  62.9 2.0 multiply_add_fusion.1
  66.6 0.8 convolution_add_fusion.3
  68.3 12.5 %fusion.34 = f32[16,128,32]{1,2,0:T(8,128)S(1)} fusion(f32[16,64,128]{2,1,0:T(8,128)S(1)} %convolution_add_fusion.3, f32[16,64,128]{2,1,0:T(8,128)S(1)} %convolution_subtract_fusion.3, f32[64,128]{1,0:T(8,128)S(1)} %get-tuple-element.72, f32[64,128]{1,0:T(8,128)S(1)} %get-tuple-element.73, f32[64,64]{0,1:T(8,128)S(1)} %copy-done.15), kind=kOutput, calls=%fused_computation.82 | convolution fusion | flops 50724864 | bytes 1392640 | tf_op jit(solution)/shard_map/nk,ckm->cnm/dot_general | solution.py:85
  80.7 1.2 fusion.8
  82.0 1.7 div.37
  83.7 1.9 fusion.99
  86.4 0.8 convolution_add_fusion.1
  88.6 1.2 fusion.6
  89.8 1.7 div.40
  91.6 2.8 fusion.46
  94.3 4.4 %all-to-all-start.1 = ((bf16[16,16,256]{2,0,1:T(8,128)(2,1)}), bf16[16,16,256]{2,0,1:T(8,128)(2,1)S(1)}, u32[]{:S(2)}, u32[]{:S(2)}) async-start(bf16[16,16,256]{2,0,1:T(8,128)(2,1)} %get-tuple-element.51), calls=%async_computation.1 | async-start | bytes 262144 | tf_op jit(solution)/shard_map/all_to_all | solution.py:135
  100.4 0.8 convolution_add_fusion
  103.8 4.3 %convolution_multiply_fusion = f32[4096,64]{0,1:T(8,128)S(1)} fusion(f32[64,16]{0,1:T(8,128)S(1)} %copy-done.33, f32[4096,64]{0,1:T(8,128)S(1)} %copy-done.5, f32[2,8,32,128]{3,2,1,0:T(8,128)S(1)} %bitcast.199, f32[4096]{0:T(1024)S(1)} %convert_multiply_fusion.5, f32[16]{0:T(128)S(1)} %copy-done.36), kind=kOutput, calls=%fused_computation | convolution fusion | flops 50790400 | bytes 2379840 | tf_op jit(solution)/shard_map/fc,ct->ft/dot_general | solution.py:148
  108.1 1.0 fusion.38
  109.1 102.5 %psum.15 = f32[33,64]{1,0:T(8,128)S(1)} all-reduce(f32[33,64]{1,0:T(8,128)S(1)} %fusion.38), channel_id=1, replica_groups=mesh['ctx'=16,'chan'=32] {'ctx','chan'}, use_global_device_ids=true, to_apply=%region_8.9 | all-reduce | flops 2112 | bytes 16896 | tf_op jit(solution)/shard_map/psum | solution.py:171
  212.2 1.7 convolution_multiply_fusion.1
  213.8 8.0 %all-to-all-start.3 = ((bf16[16,16,256]{2,0,1:T(8,128)(2,1)}), bf16[16,16,256]{2,0,1:T(8,128)(2,1)S(1)}, u32[]{:S(2)}, u32[]{:S(2)}) async-start(bf16[16,16,256]{2,0,1:T(8,128)(2,1)} %get-tuple-element.52), calls=%async_computation.3 | async-start | bytes 262144 | tf_op jit(solution)/shard_map/all_to_all | solution.py:151
  222.4 1.6 fusion.42
  224.0 5.3 %all-to-all-done.3 = bf16[16,16,256]{2,0,1:T(8,128)(2,1)S(1)} async-done(((bf16[16,16,256]{2,0,1:T(8,128)(2,1)}), bf16[16,16,256]{2,0,1:T(8,128)(2,1)S(1)}, u32[]{:S(2)}, u32[]{:S(2)}) %all-to-all-start.3) | async-done | bytes 131104 | tf_op jit(solution)/shard_map/all_to_all | solution.py:151
  229.3 2.1 multiply_reduce_fusion
  231.5 4.1 %collective-permute-start.1 = (f32[3,256,6]{2,1,0:T(8,128)S(1)}, f32[3,256,6]{2,1,0:T(8,128)S(1)}, u32[]{:S(2)}, u32[]{:S(2)}) collective-permute-start(f32[3,256,6]{2,1,0:T(8,128)S(1)} %slice.180), channel_id=1, source_target_pairs={{32,0},{64,32},{96,64},{128,96},{160,128},{192,160},{224,192},{256... | collective-permute-start | bytes 55304 | tf_op jit(solution)/shard_map/ppermute | solution.py:17
  235.6 64.1 %psum.14 = f32[3,7,256]{2,0,1:T(4,128)S(1)} all-reduce(f32[3,7,256]{2,0,1:T(4,128)S(1)} %constant_dynamic-update-slice_fusion), channel_id=1, replica_groups=mesh['ctx'=16,'chan'=32] {'ctx'}, use_global_device_ids=true, to_apply=%region_7.8 | all-reduce | flops 5376 | bytes 43008 | tf_op jit(solution)/shard_map/psum | solution.py:170
  301.0 2.1 fusion.11
  (130 shorter events, 18.6 us)
Async XLA Ops:
  0.6 6.2 %copy-start = (f32[33,64]{1,0:T(8,128)S(1)}, f32[33,64]{1,0:T(8,128)}, u32[]{:S(2)}) copy-start(f32[33,64]{1,0:T(8,128)} %param.14) | copy-start | bytes 25348
  0.6 6.2 %copy-start.39 = (f32[16]{0:T(128)S(1)}, f32[16]{0:T(128)}, u32[]{:S(2)}) copy-start(f32[16]{0:T(128)} %param.16) | copy-start | bytes 196
  1.7 17.1 %collective-permute-start = (bf16[3,256,6]{2,1,0:T(8,128)(2,1)S(1)}, bf16[3,256,6]{2,1,0:T(8,128)(2,1)S(1)}, u32[]{:S(2)}, u32[]{:S(2)}) collective-permute-start(bf16[3,256,6]{2,1,0:T(8,128)(2,1)S(1)} %pad_maximum_fusion.5), channel_id=1, source_target_pairs={{0,32},{32,64},{64,96},{96,128},{128,160},{160,192},{192,224},{224... | collective-permute-start | bytes 27656 | tf_op jit(solution)/shard_map/ppermute | solution.py:17
  5.3 8.6 %copy-start.13 = (f32[64,64]{0,1:T(8,128)}, f32[64,64]{0,1:T(8,128)S(1)}, u32[]{:S(2)}) copy-start(f32[64,64]{0,1:T(8,128)S(1)} %fusion.157) | copy-start | bytes 49156
  5.7 6.9 %copy-start.22 = (f32[1,4096]{1,0:T(1,128)}, f32[1,4096]{1,0:T(1,128)S(1)}, u32[]{:S(2)}) copy-start(f32[1,4096]{1,0:T(1,128)S(1)} %convert_multiply_fusion.6) | copy-start | bytes 49156
  6.8 5.8 %copy-start.6 = (f32[16,4096]{1,0:T(8,128)}, f32[16,4096]{1,0:T(8,128)S(1)}, u32[]{:S(2)}) copy-start(f32[16,4096]{1,0:T(8,128)S(1)} %get-tuple-element.62) | copy-start | bytes 786436
  6.8 5.8 %copy-start.8 = (f32[16,4096]{1,0:T(8,128)}, f32[16,4096]{1,0:T(8,128)S(1)}, u32[]{:S(2)}) copy-start(f32[16,4096]{1,0:T(8,128)S(1)} %get-tuple-element.63) | copy-start | bytes 786436
  6.8 5.7 %copy-start.35 = (f32[16]{0:T(128)}, f32[16]{0:T(128)S(1)}, u32[]{:S(2)}) copy-start(f32[16]{0:T(128)S(1)} %neg.24) | copy-start | bytes 196
  6.9 5.7 %copy-start.32 = (f32[64,16]{0,1:T(8,128)S(1)}, f32[64,16]{0,1:T(8,128)}, u32[]{:S(2)}) copy-start(f32[64,16]{0,1:T(8,128)} %param.15) | copy-start | bytes 12292
  15.4 1.6 copy-start.34
  17.0 1.8 copy-start.18
  17.0 1.8 copy-start.19
  17.0 1.8 copy-start.20
  18.7 2.5 copy-start.24
  18.7 2.5 copy-start.26
  18.8 2.5 copy-start.28
  18.8 2.5 copy-start.30
  21.3 0.9 copy-start.1
  22.8 15.2 %all-to-all-start = ((bf16[16,16,256]{2,1,0:T(8,128)(2,1)}), bf16[16,16,256]{2,1,0:T(8,128)(2,1)S(1)}, u32[]{:S(2)}, u32[]{:S(2)}) async-start(bf16[16,16,256]{2,1,0:T(8,128)(2,1)} %bitcast.202), calls=%async_computation | async-start | bytes 262144 | tf_op jit(solution)/shard_map/all_to_all | solution.py:119
  30.5 2.7 copy-start.21
  33.2 10.9 %copy-start.14 = (f32[64,64]{0,1:T(8,128)S(1)}, f32[64,64]{0,1:T(8,128)}, u32[]{:S(2)}) copy-start(f32[64,64]{0,1:T(8,128)} %copy-done.13) | copy-start | bytes 49156
  38.1 12.8 %all-to-all-start.2 = ((bf16[16,16,256]{2,1,0:T(8,128)(2,1)}), bf16[16,16,256]{2,1,0:T(8,128)(2,1)}, u32[]{:S(2)}, u32[]{:S(2)}) async-start(bf16[16,16,256]{2,1,0:T(8,128)(2,1)} %bitcast.22), calls=%async_computation.2 | async-start | bytes 262144 | tf_op jit(solution)/shard_map/all_to_all | solution.py:136
  43.5 0.7 copy-start.12
  61.7 1.0 copy-start.10
  61.7 1.2 copy-start.11
  67.4 0.8 copy-start.15
  83.7 1.9 copy-start.4
  85.6 1.7 copy-start.3
  87.3 0.8 copy-start.16
  94.3 119.5 %all-to-all-start.1 = ((bf16[16,16,256]{2,0,1:T(8,128)(2,1)}), bf16[16,16,256]{2,0,1:T(8,128)(2,1)S(1)}, u32[]{:S(2)}, u32[]{:S(2)}) async-start(bf16[16,16,256]{2,0,1:T(8,128)(2,1)} %get-tuple-element.51), calls=%async_computation.1 | async-start | bytes 262144 | tf_op jit(solution)/shard_map/all_to_all | solution.py:135
  101.2 0.8 copy-start.17
  102.5 1.2 copy-start.5
  102.5 1.2 copy-start.33
  102.5 1.2 copy-start.36
  103.8 4.3 %copy-start.7 = (f32[16,4096]{1,0:T(8,128)S(1)}, f32[16,4096]{1,0:T(8,128)}, u32[]{:S(2)}) copy-start(f32[16,4096]{1,0:T(8,128)} %copy-done.6) | copy-start | bytes 786436
  103.8 4.3 %copy-start.9 = (f32[16,4096]{1,0:T(8,128)S(1)}, f32[16,4096]{1,0:T(8,128)}, u32[]{:S(2)}) copy-start(f32[16,4096]{1,0:T(8,128)} %copy-done.8) | copy-start | bytes 786436
  103.8 4.3 %copy-start.23 = (f32[1,4096]{1,0:T(1,128)S(1)}, f32[1,4096]{1,0:T(1,128)}, u32[]{:S(2)}) copy-start(f32[1,4096]{1,0:T(1,128)} %copy-done.22) | copy-start | bytes 49156
  108.1 104.1 %copy-start.37 = (f32[16]{0:T(128)S(1)}, f32[16]{0:T(128)}, u32[]{:S(2)}) copy-start(f32[16]{0:T(128)} %copy-done.35) | copy-start | bytes 196
  109.1 112.8 %copy-start.38 = (f32[16]{0:T(128)S(1)}, f32[16]{0:T(128)}, u32[]{:S(2)}) copy-start(f32[16]{0:T(128)} %get-tuple-element.50) | copy-start | bytes 196
  109.1 113.3 %copy-start.2 = (f32[3,256,256]{2,1,0:T(8,128)S(1)}, f32[3,256,256]{2,1,0:T(8,128)}, u32[]{:S(2)}) copy-start(f32[3,256,256]{2,1,0:T(8,128)} %copy-done.1) | copy-start | bytes 2359300
  213.8 15.5 %all-to-all-start.3 = ((bf16[16,16,256]{2,0,1:T(8,128)(2,1)}), bf16[16,16,256]{2,0,1:T(8,128)(2,1)S(1)}, u32[]{:S(2)}, u32[]{:S(2)}) async-start(bf16[16,16,256]{2,0,1:T(8,128)(2,1)} %get-tuple-element.52), calls=%async_computation.3 | async-start | bytes 262144 | tf_op jit(solution)/shard_map/all_to_all | solution.py:151
  231.5 68.8 %collective-permute-start.1 = (f32[3,256,6]{2,1,0:T(8,128)S(1)}, f32[3,256,6]{2,1,0:T(8,128)S(1)}, u32[]{:S(2)}, u32[]{:S(2)}) collective-permute-start(f32[3,256,6]{2,1,0:T(8,128)S(1)} %slice.180), channel_id=1, source_target_pairs={{32,0},{64,32},{96,64},{128,96},{160,128},{192,160},{224,192},{256... | collective-permute-start | bytes 55304 | tf_op jit(solution)/shard_map/ppermute | solution.py:17
  300.3 0.7 copy-start.25
  300.3 0.7 copy-start.27
  300.3 0.7 copy-start.29
  300.3 0.7 copy-start.31
where the time goes:
time: 307 us; the launch traced here: 304 us
  blocking collectives  167 us (54%)
  matrix products  60.7 us (20%)
  starting transfers between devices  32.9 us (11%)
  other arithmetic  17.2 us (6%)
  waiting for transfers between devices  13.5 us (4%)
  local copies, waits for them, and re-layouts  11.6 us (4%)
    psum x1, blocking collectives, per_device(): in_total = lax.psum(in_part, ('ctx', 'chan'))  102 us
    psum x1, blocking collectives, per_device(): tap_total = lax.psum(tap_local, 'ctx')  64.1 us
    dot_general x3, matrix products, signal_of(): jnp.einsum('nk,ckm->cnm', cos_first[:half, :], real_d, precision=HIGH)  13.5 us
    all_to_all x1, starting transfers between devices, per_device(): lax.all_to_all(back_cols, 'ctx', split_axis=1, concat_axis=0, tiled=True)  8.01 us
    all_to_all x1, starting transfers between devices, per_device(): lax.all_to_all(mixer_in, 'ctx', split_axis=0, concat_axis=1, tiled=True)  7.67 us
    ppermute x2, starting transfers between devices, shifted(): return lax.ppermute(x, axis, pairs)  7.56 us
  transfers between devices with their start and end apart: 6, of which 3 were waited for; matrix products, arithmetic and copies ran while one was open for 11% of the time, Pallas kernels for 0%

commit v1 on v0

v1 whole, which is shorter than its diff:
```python
import functools
import math

import jax
import jax.numpy as jnp
import ml_dtypes
import numpy as np
from jax import lax
from jax.experimental import pallas as pl
from jax.experimental.pallas import tpu as pltpu
from jax.sharding import PartitionSpec as P

D = 8192
SEQ = 4096
EMB = 33
FH = 64
TAPS = 7
NCTX = 16
POS = SEQ // NCTX
OWN = 16
K1 = 40
N1 = 64
N2 = 128
BLK = SEQ // N2
FEAT = 48
MESH = pl.DeviceIdType.MESH
f32 = jnp.float32
bf16 = jnp.bfloat16


def halves(x):
    x = np.asarray(x, np.float32)
    hi = x.astype(ml_dtypes.bfloat16)
    lo = (x - hi.astype(np.float32)).astype(ml_dtypes.bfloat16)
    return hi, lo


def tables():
    k1 = np.arange(K1)[:, None]
    live = (k1 <= N1 // 2).astype(np.float64)
    n = np.arange(BLK)[None, :]
    ang = 2 * np.pi * ((k1 * n) % N1) / N1
    c1 = np.concatenate([np.cos(ang) * live, -np.sin(ang) * live], 0)
    hi, lo = halves(c1)
    c1_two = np.concatenate([hi, lo], 1)
    c1_three = np.concatenate([hi, hi, lo], 1)
    weight = np.where((k1 == 0) | (k1 == N1 // 2), 1.0, 2.0) * live / (N1 * N2)
    d1 = np.concatenate([np.cos(ang) * weight, -np.sin(ang) * weight], 0).T
    hi, lo = halves(d1)
    d1_three = np.concatenate([hi, hi, lo], 1)
    m = np.arange(N2)
    turn = 2 * np.pi * ((m[:, None] * m[None, :]) % N2) / N2
    c, s = np.cos(turn), np.sin(turn)
    fwd = np.block([[c, -s], [s, c]])
    hi, lo = halves(fwd)
    fwd_three = np.concatenate([hi, hi, lo], 0)
    hi, lo = halves(fwd.T)
    inv_three = np.concatenate([hi, hi, lo], 0)
    twist = 2 * np.pi * ((k1 * m[None, :]) % (N1 * N2)) / (N1 * N2)
    twist = np.concatenate([np.cos(twist), np.sin(twist)], 0).astype(np.float32)
    t = np.arange(SEQ)
    bands = (EMB - 1) // 2
    b = np.arange(1, bands + 1)
    phase = 2 * np.pi * ((b[:, None] * t[None, :]) % SEQ) / SEQ
    feat = np.zeros((FEAT, SEQ))
    feat[0] = t / SEQ
    feat[1 : 1 + bands] = np.cos(phase)
    feat[1 + bands : 1 + 2 * bands] = np.sin(phase)
    feat_hi, feat_lo = halves(feat)
    tail = np.zeros((32, 3 * 128), np.float32)
    head = np.zeros((48, 6 * 128), np.float32)
    place = np.zeros((48, 3 * 128), np.float32)
    for i in range(3):
        for r in range(8):
            tail[i * 8 + r, i * 128 + 120 + r] = 1
            for h in range(2):
                head[i * 16 + h * 8 + r, (i * 2 + h) * 128 + r] = 1
                place[i * 16 + h * 8 + r, i * 128 + r] = 1
    as16 = lambda x: x.astype(ml_dtypes.bfloat16)
    return (c1_two, c1_three, d1_three, fwd_three, inv_three, twist, feat_hi, feat_lo,
            as16(tail), as16(head), as16(place))


def split(x):
    hi = x.astype(bf16)
    return hi, (x - hi.astype(f32)).astype(bf16)


def mm(a, b, ca=1, cb=0):
    return lax.dot_general(a, b, (((ca,), (cb,)), ((), ())), preferred_element_type=f32)


def sin_cos(x):
    n = jnp.floor(x * (1.0 / math.pi) + 0.5)
    r = x - n * 3.140625
    r = r - n * 9.67502593994140625e-4
    r = r - n * 1.509957990978376e-7
    sign = 1.0 - 2.0 * (n - 2.0 * jnp.floor(n * 0.5))
    z = r * r
    s = -1.0 / 39916800.0
    for k in (1.0 / 362880.0, -1.0 / 5040.0, 1.0 / 120.0, -1.0 / 6.0, 1.0):
        s = s * z + k
    c = 1.0 / 479001600.0
    for k in (-1.0 / 3628800.0, 1.0 / 40320.0, -1.0 / 720.0, 1.0 / 24.0, -0.5, 1.0):
        c = c * z + k
    return s * r * sign, c * sign


def kernel(quads, stacks,
           q_ref, k_ref, v_ref, cot_ref, taps_ref, fin_ref, fout_ref, decay_ref, skip_ref,
           c1_two, c1_three, d1_three, fwd_three, inv_three, twist, feat_hi, feat_lo,
           tail_sel, head_sel, head_place,
           mixed_ref, qg_ref, kg_ref, vg_ref, tg_ref, fig_ref, fog_ref, sg_ref,
           tails_out, tails_in, heads_out, heads_in, tap_rows, tap_cols, fin_pad,
           prev, shorts, shifted, grads, ahead, bend, act_hi, act_lo, env,
           sig, sig_u, spec_h, spec_u, spec_g,
           ug_out, ug_in, conv_out, conv_in, back_out, back_in, bent_hi, bent_lo,
           prods, tap_tiles, tap_parts, tap_sums, in_tiles, in_parts, in_mine,
           in_quad, in_next, in_stack, in_sums, in_flat,
           halo_s, halo_r, ug_s, ug_r, conv_s, conv_r, back_s, back_r,
           tp_s, tp_r, ts_s, ts_r, ip_s, ip_r, iq_s, iq_r, iz_s, iz_r, is_s, is_r):
    me = lax.axis_index("ctx")
    ch = lax.axis_index("chan")
    layer = ch // quads
    member = ch % quads

    def at(ctx_index):
        return {"ctx": ctx_index, "chan": ch}

    def over(chan_index):
        return {"ctx": me, "chan": chan_index}

    def copy(src, dst, send, recv, where):
        return pltpu.make_async_remote_copy(
            src_ref=src, dst_ref=dst, send_sem=send, recv_sem=recv,
            device_id=where, device_id_type=MESH)

    def each(count, body, start=1):
        def step(d, carry):
            body(d)
            return carry
        if count > start:
            lax.fori_loop(start, count, step, 0)

    def other(d):
        return lax.rem(me + d, NCTX)

    def quad_peer(d):
        return layer * quads + lax.rem(member + d, quads)

    def stack_peer(d):
        return lax.rem(layer + d, stacks) * quads + member

    barrier = pltpu.get_barrier_semaphore()

    def greet(where):
        pl.semaphore_signal(barrier, inc=1, device_id=where, device_id_type=MESH)

    each(NCTX, lambda d: greet(at(other(d))))
    each(quads, lambda d: greet(over(quad_peer(d))))
    each(stacks, lambda d: greet(over(stack_peer(d))))

    ends = jnp.concatenate([r[:, 128:256] for r in (q_ref, k_ref, v_ref)], axis=1)
    tails_out[...] = mm(tail_sel[...], ends, 1, 1).astype(bf16)
    pl.semaphore_wait(barrier, NCTX - 1 + (quads - 1) + (stacks - 1))
    tail_copy = copy(tails_out, tails_in, halo_s.at[0], halo_r.at[0], at(other(1)))
    tail_copy.start()

    tap_rows[...] = jnp.zeros_like(tap_rows)
    for i in range(3):
        tap_rows[i * 8 : i * 8 + TAPS, :] = taps_ref[i]
    row = lax.broadcasted_iota(jnp.int32, (24, 128), 0)
    col = lax.broadcasted_iota(jnp.int32, (24, 128), 1)
    unit = (row == col).astype(bf16)
    hi, lo = split(tap_rows[...])
    rest = (tap_rows[...] - hi.astype(f32) - lo.astype(f32)).astype(bf16)
    tap_cols[...] = mm(hi, unit, 0, 0) + mm(lo, unit, 0, 0) + mm(rest, unit, 0, 0)

    fin_pad[...] = jnp.zeros_like(fin_pad)
    fin_pad[0:EMB, :] = fin_ref[...]
    fin_hi, fin_lo = split(fin_pad[...])
    WIDE = 512

    def network(d):
        cols = pl.ds(pl.multiple_of(d * WIDE, WIDE), WIDE)
        a, b = feat_hi[:, cols], feat_lo[:, cols]
        pre = mm(fin_hi, a, 0, 0) + mm(fin_lo, a, 0, 0) + mm(fin_hi, b, 0, 0)
        s, c = sin_cos(pre)
        bend[:, cols] = c
        a, b = split(s)
        act_hi[:, cols] = a
        act_lo[:, cols] = b

    each(SEQ // WIDE, network, 0)

    tail_copy.wait_recv()
    inside = jnp.where(me > 0, 1.0, 0.0)
    prev[...] = mm(tails_in[...], tail_sel[...], 0, 0) * inside
    ROWS = 32
    CHUNKS = 256 // ROWS

    def moved(x, by):
        return x if by == 0 else pltpu.roll(x, by, 1)

    def short_part(d):
        part = lax.rem(me // 2 + d, CHUNKS)
        rows = pl.ds(pl.multiple_of(part * ROWS, ROWS), ROWS)
        res = []
        for i, ref in enumerate((q_ref, k_ref, v_ref)):
            x = jnp.concatenate(
                [prev[rows, i * 128 : (i + 1) * 128], ref[rows, :].astype(f32)], axis=1)
            acc = None
            for j in range(TAPS):
                term = tap_cols[rows, i * 8 + j : i * 8 + j + 1] * moved(x, j)[:, 128:384]
                acc = term if acc is None else acc + term
            shorts[i, rows, :] = acc
            res.append(acc)
        u = (res[1] * res[2]).astype(bf16)
        g = (cot_ref[rows, :].astype(f32) * res[0]).astype(bf16)
        for h in range(2):
            p = part * 2 + h
            ug_out[p, 0:16, :] = u[h * 16 : (h + 1) * 16, :]
            ug_out[p, 16:32, :] = g[h * 16 : (h + 1) * 16, :]

            @pl.when(p != me)
            def _():
                copy(ug_out.at[p], ug_in.at[me], ug_s.at[p], ug_r.at[me], at(p)).start()

    each(CHUNKS, short_part, 0)
    ug_in[me] = ug_out[me]

    eye = (lax.broadcasted_iota(jnp.int32, (OWN, OWN), 0)
           == lax.broadcasted_iota(jnp.int32, (OWN, OWN), 1)).astype(f32)
    decay = jnp.sum(eye * decay_ref[...], axis=1, keepdims=True)
    skip = jnp.sum(eye * skip_ref[...], axis=1, keepdims=True)
    w_hi, w_lo = split(fout_ref[...])
    scale = 1.0 / math.sqrt(SEQ)

    def filters(d):
        cols = pl.ds(pl.multiple_of(d * WIDE, WIDE), WIDE)
        a, b = act_hi[:, cols], act_lo[:, cols]
        raw = mm(w_hi, a, 0, 0) + mm(w_lo, a, 0, 0) + mm(w_hi, b, 0, 0)
        t = (d * WIDE + lax.broadcasted_iota(jnp.int32, (OWN, WIDE), 1)).astype(f32)
        e = jnp.exp(-decay * (t * (1.0 / SEQ))) * scale
        h = raw * e
        for n in range(WIDE // 128):
            rows = pl.ds(pl.multiple_of((d * (WIDE // 128) + n) * OWN, OWN), OWN)
            env[rows, :] = e[:, n * 128 : (n + 1) * 128]
            sig[rows, :] = h[:, n * 128 : (n + 1) * 128]

    each(SEQ // WIDE, filters, 0)

    GRP = 4
    tc, ts = twist[0:K1, :], twist[K1 : 2 * K1, :]

    def three(x, axis):
        hi, lo = split(x)
        return jnp.concatenate([hi, lo, hi], axis=axis)

    def forward(src, spec, exact):
        for grp in range(OWN // GRP):
            x = jnp.concatenate(
                [src[pl.ds(grp * GRP + c, BLK, stride=OWN), :] for c in range(GRP)], axis=1)
            if exact:
                x = x.astype(bf16)
                a = mm(c1_two[...], jnp.concatenate([x, x], axis=0))
            else:
                a = mm(c1_three[...], three(x, 0))
            re, im = [], []
            for c in range(GRP):
                ar = a[0:K1, c * 128 : (c + 1) * 128]
                ai = a[K1 : 2 * K1, c * 128 : (c + 1) * 128]
                re.append(ar * tc + ai * ts)
                im.append(ai * tc - ar * ts)
            x = jnp.concatenate([jnp.concatenate(re, 0), jnp.concatenate(im, 0)], axis=1)
            spec[grp * GRP * K1 : (grp + 1) * GRP * K1, :] = mm(three(x, 1), fwd_three[...])

    def backward(first, second, conj, dst):
        for grp in range(OWN // GRP):
            rows = slice(grp * GRP * K1, (grp + 1) * GRP * K1)
            ar, ai = first[rows, 0:128], first[rows, 128:256]
            br, bi = second[rows, 0:128], second[rows, 128:256]
            if conj:
                y = [ar * br + ai * bi, ai * br - ar * bi]
            else:
                y = [ar * br - ai * bi, ar * bi + ai * br]
            z = mm(three(jnp.concatenate(y, axis=1), 1), inv_three[...])
            out = []
            for c in range(GRP):
                zr = z[c * K1 : (c + 1) * K1, 0:128]
                zi = z[c * K1 : (c + 1) * K1, 128:256]
                out.append(jnp.concatenate([zr * tc - zi * ts, zi * tc + zr * ts], axis=0))
            r = mm(d1_three[...], three(jnp.concatenate(out, axis=1), 0))
            for c in range(GRP):
                dst[pl.ds(grp * GRP + c, BLK, stride=OWN), :] = r[:, c * 128 : (c + 1) * 128]

    forward(sig, spec_h, False)

    def shift_part(d):
        rows = pl.ds(pl.multiple_of(d * ROWS, ROWS), ROWS)
        for i, ref in enumerate((q_ref, k_ref, v_ref)):
            x = jnp.concatenate(
                [prev[rows, i * 128 : (i + 1) * 128], ref[rows, :].astype(f32)], axis=1)
            for j in range(TAPS):
                shifted[i * TAPS + j, rows, :] = moved(x, j)[:, 128:384].astype(bf16)

    each(CHUNKS, shift_part, 0)

    def ug_wait(d):
        p = other(d)
        copy(ug_out.at[p], ug_in.at[p], ug_s.at[p], ug_r.at[p], at(p)).wait_recv()

    each(NCTX, ug_wait)
    for s in range(NCTX):
        for h in range(2):
            n = 2 * s + h
            sig_u[n * 16 : (n + 1) * 16, :] = ug_in[s, 0:16, h * 128 : (h + 1) * 128].astype(f32)
            sig[n * 16 : (n + 1) * 16, :] = ug_in[s, 16:32, h * 128 : (h + 1) * 128].astype(f32)
    forward(sig_u, spec_u, True)
    forward(sig, spec_g, True)

    def scatter(result, first_row, out, inn, send, recv):
        for s in range(NCTX):
            x = jnp.concatenate(
                [result[(2 * s + h) * 16 : (2 * s + h + 1) * 16, :] for h in range(2)], axis=1)
            x = x + skip * ug_in[s, first_row : first_row + 16, :].astype(f32)
            out[s] = x.astype(bf16)
        mine = pl.ds(pl.multiple_of(me * 16, 16), 16)
        inn[mine, :] = out[me]

        def go(d):
            p = other(d)
            copy(out.at[p], inn.at[mine, :], send.at[p], recv.at[me], at(p)).start()

        each(NCTX, go)

    backward(spec_u, spec_h, False, sig_u)
    scatter(sig_u, 0, conv_out, conv_in, conv_s, conv_r)
    backward(spec_g, spec_h, True, sig)
    scatter(sig, 16, back_out, back_in, back_s, back_r)

    backward(spec_g, spec_u, True, sig)
    sg_ref[...] = jnp.sum(eye * sig[0:16, 0:1], axis=0, keepdims=True) * scale
    for n in range(BLK):
        a, b = split(sig[n * 16 : (n + 1) * 16, :] * env[n * 16 : (n + 1) * 16, :])
        bent_hi[:, n * 128 : (n + 1) * 128] = a
        bent_lo[:, n * 128 : (n + 1) * 128] = b

    def gradient(d, carry):
        out_sum, in_sum = carry
        cols = pl.ds(pl.multiple_of(d * WIDE, WIDE), WIDE)
        bh, bl = bent_hi[:, cols], bent_lo[:, cols]
        ah, al = act_hi[:, cols], act_lo[:, cols]
        out_sum = out_sum + mm(ah, bh, 1, 1) + mm(al, bh, 1, 1) + mm(ah, bl, 1, 1)
        slope = (mm(w_hi, bh) + mm(w_lo, bh) + mm(w_hi, bl)) * bend[:, cols]
        sh, sl = split(slope)
        fh, fl = feat_hi[:, cols], feat_lo[:, cols]
        in_sum = in_sum + mm(fh, sh, 1, 1) + mm(fl, sh, 1, 1) + mm(fh, sl, 1, 1)
        return out_sum, in_sum

    out_sum, in_sum = lax.fori_loop(
        0, SEQ // WIDE, gradient, (jnp.zeros((FH, OWN), f32), jnp.zeros((FEAT, FH), f32)))
    fog_ref[...] = out_sum * scale
    in_flat[...] = jnp.zeros_like(in_flat)
    in_flat[:, 0:FH] = in_sum
    packed = in_flat[0:24, :] + pltpu.roll(in_flat[24:48, :], 64, 1)
    for k in range(3):
        in_tiles[k] = packed[k * 8 : (k + 1) * 8, :]

    def deal(count, odd, tiles, parts, send, recv, go):
        for k in range(count):
            @pl.when(me != 2 * k + odd)
            def _(k=k):
                c = copy(tiles.at[k], parts.at[me], send.at[k], recv.at[me], at(2 * k + odd))
                go(c)

    deal(3, 1, in_tiles, in_parts, ip_s, ip_r, lambda c: c.start())
    in_owner = jnp.logical_and(lax.rem(me, 2) == 1, me < 6)
    tap_owner = jnp.logical_and(lax.rem(me, 2) == 0, me < 12)
    in_index = jnp.minimum(me // 2, 2)
    tap_index = jnp.minimum(me // 2, 5)

    def rows_wait(out, inn, send, recv):
        def one(d):
            p = other(d)
            rows = pl.ds(pl.multiple_of(p * 16, 16), 16)
            copy(out.at[p], inn.at[rows, :], send.at[p], recv.at[p], at(p)).wait_recv()
        each(NCTX, one)

    rows_wait(conv_out, conv_in, conv_s, conv_r)
    rows_wait(back_out, back_in, back_s, back_r)

    def grad_part(d):
        rows = pl.ds(pl.multiple_of(d * ROWS, ROWS), ROWS)
        cv = conv_in[rows, :].astype(f32)
        bk = back_in[rows, :].astype(f32)
        mixed_ref[rows, :] = (shorts[0, rows, :] * cv).astype(bf16)
        gs = (cot_ref[rows, :].astype(f32) * cv, bk * shorts[2, rows, :], bk * shorts[1, rows, :])
        for i in range(3):
            grads[i, rows, :] = gs[i]
            hi, lo = split(gs[i][:, 0:128])
            ahead[rows, i * 256 : i * 256 + 128] = hi
            ahead[rows, i * 256 + 128 : i * 256 + 256] = lo

    each(CHUNKS, grad_part, 0)
    heads_out[...] = mm(head_sel[...], ahead[...], 1, 1).astype(bf16)
    head_copy = copy(heads_out, heads_in, halo_s.at[1], halo_r.at[1], at(other(NCTX - 1)))
    head_copy.start()

    def collect(parts, tiles, index, recv, sender_count):
        def one(d):
            p = other(d)
            copy(tiles.at[0], parts.at[p], recv.at[p], recv.at[p], at(p)).wait_recv()
        each(NCTX, one)
        parts[me] = tiles[index]
        total = parts[0]
        for p in range(1, sender_count):
            total = total + parts[p]
        return total

    @pl.when(in_owner)
    def _():
        in_quad[member] = collect(in_parts, in_tiles, in_index, ip_r, NCTX)

        def go(d):
            p = quad_peer(d)
            copy(in_quad.at[member], in_quad.at[member], iq_s.at[d], iq_r.at[member],
                 over(p)).start()
        each(quads, go)

    def prod_part(d):
        rows = pl.ds(pl.multiple_of(d * ROWS, ROWS), ROWS)
        for i in range(3):
            g = grads[i, rows, :]
            for j in range(TAPS):
                x = g * shifted[i * TAPS + j, rows, :].astype(f32)
                hi, lo = split(x[:, 0:128] + x[:, 128:256])
                prods[i * TAPS + j, rows, 0:128] = hi
                prods[i * TAPS + j, rows, 128:256] = lo

    each(CHUNKS, prod_part, 0)
    pick_row = lax.broadcasted_iota(jnp.int32, (32, 256), 0)
    total = jnp.zeros((32, 256), f32)
    for i in range(3):
        for j in range(TAPS):
            pick = (pick_row == i * 8 + j).astype(f32).astype(bf16)
            total = total + mm(pick, prods[i * TAPS + j], 1, 1)
    for k in range(6):
        tap_tiles[k] = total[(k // 2) * 8 : (k // 2) * 8 + 8, (k % 2) * 128 : (k % 2) * 128 + 128]
    deal(6, 0, tap_tiles, tap_parts, tp_s, tp_r, lambda c: c.start())

    @pl.when(in_owner)
    def _():
        def one(d):
            p = lax.rem(member + d, quads)
            copy(in_quad.at[p], in_quad.at[p], iq_s.at[d], iq_r.at[p], over(quad_peer(d))).wait_recv()
        each(quads, one)
        t = in_quad[0]
        for p in range(1, quads):
            t = t + in_quad[p]
        in_stack[layer] = t

        def go(d):
            copy(in_stack.at[layer], in_stack.at[layer], iz_s.at[d], iz_r.at[layer],
                 over(stack_peer(d))).start()
        each(stacks, go)

    head_copy.wait_recv()
    before_end = jnp.where(me < NCTX - 1, 1.0, 0.0)
    prev[...] = mm(heads_in[...], head_place[...], 0, 0) * before_end

    def proj_part(d):
        rows = pl.ds(pl.multiple_of(d * ROWS, ROWS), ROWS)
        for i, ref in enumerate((qg_ref, kg_ref, vg_ref)):
            x = jnp.concatenate([grads[i, rows, :], prev[rows, i * 128 : (i + 1) * 128]], axis=1)
            acc = None
            for j in range(TAPS):
                y = moved(x, (384 - j) % 384)[:, 0:256]
                term = tap_cols[rows, i * 8 + j : i * 8 + j + 1] * y
                acc = term if acc is None else acc + term
            ref[rows, :] = acc.astype(bf16)

    each(CHUNKS, proj_part, 0)

    @pl.when(tap_owner)
    def _():
        tap_sums[tap_index] = collect(tap_parts, tap_tiles, tap_index, tp_r, NCTX)

        def go(d):
            copy(tap_sums.at[tap_index], tap_sums.at[tap_index], ts_s.at[d], ts_r.at[tap_index],
                 at(other(d))).start()
        each(NCTX, go)

    @pl.when(in_owner)
    def _():
        def one(d):
            p = lax.rem(layer + d, stacks)
            copy(in_stack.at[p], in_stack.at[p], iz_s.at[d], iz_r.at[p], over(stack_peer(d))).wait_recv()
        each(stacks, one)
        t = in_stack[0]
        for p in range(1, stacks):
            t = t + in_stack[p]
        in_sums[in_index] = t

        def go(d):
            copy(in_sums.at[in_index], in_sums.at[in_index], is_s.at[d], is_r.at[in_index],
                 at(other(d))).start()
        each(NCTX, go)

    for k in range(6):
        @pl.when(me != 2 * k)
        def _(k=k):
            copy(tap_sums.at[k], tap_sums.at[k], ts_s.at[0], ts_r.at[k], at(2 * k)).wait_recv()
    for i in range(3):
        both = jnp.concatenate([tap_sums[2 * i], tap_sums[2 * i + 1]], axis=1) * scale
        tg_ref[i] = both[0:TAPS, :]
    for k in range(3):
        @pl.when(me != 2 * k + 1)
        def _(k=k):
            copy(in_sums.at[k], in_sums.at[k], is_s.at[0], is_r.at[k], at(2 * k + 1)).wait_recv()
    sums = jnp.concatenate([in_sums[k] for k in range(3)], axis=0) * (scale / math.sqrt(D))
    fig_ref[0:24, :] = sums[:, 0:FH]
    fig_ref[24:EMB, :] = pltpu.roll(sums, 64, 1)[0 : EMB - 24, 0:FH]

    tail_copy.wait_send()
    head_copy.wait_send()
    deal(3, 1, in_tiles, in_parts, ip_s, ip_r, lambda c: c.wait_send())
    deal(6, 0, tap_tiles, tap_parts, tp_s, tp_r, lambda c: c.wait_send())

    def left(d):
        p = other(d)
        mine = pl.ds(pl.multiple_of(me * 16, 16), 16)
        copy(ug_out.at[p], ug_in.at[me], ug_s.at[p], ug_r.at[me], at(p)).wait_send()
        copy(conv_out.at[p], conv_in.at[mine, :], conv_s.at[p], conv_r.at[me], at(p)).wait_send()
        copy(back_out.at[p], back_in.at[mine, :], back_s.at[p], back_r.at[me], at(p)).wait_send()

    each(NCTX, left)

    @pl.when(in_owner)
    def _():
        each(quads, lambda d: copy(in_quad.at[member], in_quad.at[member], iq_s.at[d],
                                   iq_r.at[member], over(quad_peer(d))).wait_send())
        each(stacks, lambda d: copy(in_stack.at[layer], in_stack.at[layer], iz_s.at[d],
                                    iz_r.at[layer], over(stack_peer(d))).wait_send())
        each(NCTX, lambda d: copy(in_sums.at[in_index], in_sums.at[in_index], is_s.at[d],
                                  is_r.at[in_index], at(other(d))).wait_send())

    @pl.when(tap_owner)
    def _():
        each(NCTX, lambda d: copy(tap_sums.at[tap_index], tap_sums.at[tap_index], ts_s.at[d],
                                  ts_r.at[tap_index], at(other(d))).wait_send())


def per_device(consts, chans, query_proj, key_proj, value_proj, out_cotangent, short_taps,
               filter_in, filter_out, decay_rate, skip_gain):
    quads = math.gcd(chans, 4)
    stacks = chans // quads
    vm = pl.BlockSpec(memory_space=pltpu.VMEM)
    block = jax.ShapeDtypeStruct((256, POS), bf16)
    dma = pltpu.SemaphoreType.DMA
    V = pltpu.VMEM
    args = (query_proj, key_proj, value_proj, out_cotangent, short_taps, filter_in, filter_out,
            decay_rate.reshape(1, OWN), skip_gain.reshape(1, OWN))
    outs = pl.pallas_call(
        functools.partial(kernel, quads, stacks),
        out_shape=(block, block, block, block,
                   jax.ShapeDtypeStruct((3, TAPS, 256), f32),
                   jax.ShapeDtypeStruct((EMB, FH), f32),
                   jax.ShapeDtypeStruct((FH, OWN), f32),
                   jax.ShapeDtypeStruct((1, OWN), f32)),
        in_specs=[vm] * (len(args) + len(consts)),
        out_specs=[vm] * 8,
        scratch_shapes=[
            V((32, 256), bf16), V((32, 256), bf16), V((48, 256), bf16), V((48, 256), bf16),
            V((24, 256), f32), V((256, 128), f32), V((FEAT, FH), f32),
            V((256, 384), f32), V((3, 256, 256), f32), V((21, 256, 256), bf16),
            V((3, 256, 256), f32), V((256, 768), bf16), V((FH, SEQ), f32),
            V((FH, SEQ), bf16), V((FH, SEQ), bf16), V((512, 128), f32),
            V((512, 128), f32), V((512, 128), f32),
            V((OWN * K1, 256), f32), V((OWN * K1, 256), f32), V((OWN * K1, 256), f32),
            V((NCTX, 32, 256), bf16), V((NCTX, 32, 256), bf16),
            V((NCTX, 16, 256), bf16), V((256, 256), bf16),
            V((NCTX, 16, 256), bf16), V((256, 256), bf16),
            V((OWN, SEQ), bf16), V((OWN, SEQ), bf16),
            V((21, 256, 256), bf16), V((6, 8, 128), f32), V((NCTX, 8, 128), f32),
            V((6, 8, 128), f32),
            V((3, 8, 128), f32), V((NCTX, 8, 128), f32), V((8, 128), f32),
            V((quads, 8, 128), f32), V((8, 128), f32), V((stacks, 8, 128), f32),
            V((3, 8, 128), f32), V((48, 128), f32),
            dma((2,)), dma((2,)), dma((NCTX,)), dma((NCTX,)),
            dma((NCTX,)), dma((NCTX,)), dma((NCTX,)), dma((NCTX,)),
            dma((6,)), dma((NCTX,)), dma((NCTX,)), dma((6,)),
            dma((3,)), dma((NCTX,)), dma((quads,)), dma((quads,)),
            dma((stacks,)), dma((stacks,)), dma((NCTX,)), dma((3,)),
        ],
        compiler_params=pltpu.CompilerParams(
            collective_id=0, has_side_effects=True, vmem_limit_bytes=56 * 1024 * 1024),
    )(*args, *[jnp.asarray(c) for c in consts])
    return outs[:7] + (outs[7].reshape(OWN),)


def solution(mesh):
    consts = tables()
    return jax.shard_map(
        functools.partial(per_device, consts, mesh.shape["chan"]),
        mesh=mesh,
        in_specs=(
            P("chan", "ctx"),
            P("chan", "ctx"),
            P("chan", "ctx"),
            P("chan", "ctx"),
            P(None, None, "chan"),
            P(),
            P(None, ("chan", "ctx")),
            P(("chan", "ctx")),
            P(("chan", "ctx")),
        ),
        out_specs=(
            P("chan", "ctx"),
            P("chan", "ctx"),
            P("chan", "ctx"),
            P("chan", "ctx"),
            P(None, None, "chan"),
            P(),
            P(None, ("chan", "ctx")),
            P(("chan", "ctx")),
        ),
        check_vma=False,
    )
```

time: 307 us -> 69.2 us (0.23)
  blocking collectives: 167 us -> 0 us
  matrix products: 60.7 us -> 0 us
  Pallas kernels: 0 us -> 59.1 us
  starting transfers between devices: 32.9 us -> 0 us
  other arithmetic: 17.2 us -> 0 us
  waiting for transfers between devices: 13.5 us -> 0 us
    psum x2 -> x0, blocking collectives: 167 us -> none  [the longest x1 102 us: per_device(): in_total = lax.psum(in_part, ('ctx', 'chan'))]
    dot_general x41 -> x0, matrix products: 60.7 us -> none  [the longest x3 13.5 us: signal_of(): jnp.einsum('nk,ckm->cnm', cos_first[:half, :], real_d, precision=HIGH)]
    pallas_call x0 -> x1, Pallas kernels: none -> 59.1 us  [per_device(): pl.pallas_call(functools.partial(kernel, quads, stacks), out_shape=(block...]
    all_to_all x4 -> x0, starting transfers between devices: 25.4 us -> none  [the longest x1 8.01 us: per_device(): lax.all_to_all(back_cols, 'ctx', split_axis=1, concat_axis=0, tiled=True)]
    all_to_all x4 -> x0, waiting for transfers between devices: 13.5 us -> none  [the longest x1 5.31 us: per_device(): lax.all_to_all(back_cols, 'ctx', split_axis=1, concat_axis=0, tiled=True)]
    ppermute x2 -> x0, starting transfers between devices: 7.56 us -> none  [shifted(): return lax.ppermute(x, axis, pairs)]
    unnamed x86 -> x21, local copies, waits for them, and re-layouts: 4.01 us -> 8.92 us
    reduce_sum x2 -> x0, other arithmetic: 4.88 us -> none  [the longest x1 2.76 us: per_device(): skip_local = jnp.sum(grad_f * mixer_f, axis=1) * scale]
  transfers between devices with their start and end apart: 6 -> 0, of which waited for: 3 -> 0; matrix products, arithmetic and copies ran while one was open for 11% -> 0% of each run, Pallas kernels for 0% -> 0%
where the time goes in v1:
time: 69.2 us; the launch traced here: 68.6 us
  Pallas kernels  59.1 us (85%)
  local copies, waits for them, and re-layouts  8.92 us (13%)
    pallas_call x1, Pallas kernels, per_device(): pl.pallas_call(functools.partial(kernel, quads, stacks), out_shape=(block...  59.1 us
    unnamed x21, local copies, waits for them, and re-layouts  8.92 us

profile of v1, /device:TPU:2, one launch (start us, length us, event | category | flops | bytes accessed | tf_op | source)
XLA Modules:
  0.0 68.6 jit_solution(13855651750277487743)
XLA Ops:
  0.6 1.4 %copy.28.fout_ref = f32[64,16]{1,0:T(8,128)} copy(f32[64,16]{0,1:T(8,128)} %param.26) | data formatting | bytes 8192 | tf_op args[6]
  2.0 59.1 %shard_map.251 = (bf16[256,256]{1,0:T(8,128)(2,1)}, bf16[256,256]{1,0:T(8,128)(2,1)}, bf16[256,256]{1,0:T(8,128)(2,1)}, bf16[256,256]{1,0:T(8,128)(2,1)}, f32[3,...) custom-call(bf16[256,256]{1,0:T(8,128)(2,1)} %q_ref.1, bf16[256,256]{1,0:T(8,128)(2,1)} %k_ref.1, ...), custom_call_target="tpu_custom_call" | custom-call | tf_op jit(solution)/shard_map/pallas_call | solution.py:564
  61.1 1.4 %copy.29 = f32[64,16]{0,1:T(8,128)} copy(f32[64,16]{1,0:T(8,128)} %get-tuple-element.30) | data formatting | bytes 8192
  62.5 0.0 copy-start.2
  62.5 1.6 %copy.37 = bf16[256,256]{1,0:T(8,128)(2,1)} copy(bf16[256,256]{1,0:T(8,128)(2,1)} %get-tuple-element.40) | data formatting | bytes 262144
  64.1 0.0 copy-done.2
  64.1 0.0 copy-start.1
  64.1 0.7 copy.38
  64.8 0.3 copy-done.1
  65.1 0.0 copy-start
  65.1 0.7 copy.39
  65.7 0.3 copy-done
  66.0 0.0 copy-start.3
  66.0 0.7 copy.40
  66.7 0.1 copy-done.3
  66.8 0.0 copy-start.4
  66.8 0.6 copy.41
  67.4 0.1 copy-done.4
  67.5 0.0 copy-start.5
  67.5 0.6 copy.42
  68.1 0.0 copy-done.5
  68.1 0.5 copy.43
Async XLA Ops:
  62.5 1.6 %copy-start.2 = (bf16[256,256]{1,0:T(8,128)(2,1)S(1)}, bf16[256,256]{1,0:T(8,128)(2,1)}, u32[]{:S(2)}) copy-start(bf16[256,256]{1,0:T(8,128)(2,1)} %get-tuple-element.41) | copy-start | bytes 393220
  64.1 1.0 %copy-start.1 = (bf16[256,256]{1,0:T(8,128)(2,1)S(1)}, bf16[256,256]{1,0:T(8,128)(2,1)}, u32[]{:S(2)}) copy-start(bf16[256,256]{1,0:T(8,128)(2,1)} %get-tuple-element.42) | copy-start | bytes 393220
  65.1 1.0 %copy-start = (bf16[256,256]{1,0:T(8,128)(2,1)S(1)}, bf16[256,256]{1,0:T(8,128)(2,1)}, u32[]{:S(2)}) copy-start(bf16[256,256]{1,0:T(8,128)(2,1)} %get-tuple-element.43) | copy-start | bytes 393220
  66.0 0.7 %copy-start.3 = (f32[3,7,256]{2,1,0:T(8,128)S(1)}, f32[3,7,256]{2,1,0:T(8,128)}, u32[]{:S(2)}) copy-start(f32[3,7,256]{2,1,0:T(8,128)} %get-tuple-element.44) | copy-start | bytes 64516
  66.8 0.7 %copy-start.4 = (f32[33,64]{1,0:T(8,128)S(1)}, f32[33,64]{1,0:T(8,128)}, u32[]{:S(2)}) copy-start(f32[33,64]{1,0:T(8,128)} %get-tuple-element.45) | copy-start | bytes 25348
  67.5 0.6 copy-start.5

commit v2 on v1

--- a/solution.py
+++ b/solution.py
@@ -23,6 +23,7 @@
 N2 = 128
 BLK = SEQ // N2
 FEAT = 48
+LOADS = 19
 MESH = pl.DeviceIdType.MESH
 f32 = jnp.float32
 bf16 = jnp.bfloat16
@@ -66,18 +67,19 @@
     feat[0] = t / SEQ
     feat[1 : 1 + bands] = np.cos(phase)
     feat[1 + bands : 1 + 2 * bands] = np.sin(phase)
-    feat_hi, feat_lo = halves(feat)
+    feat_two = np.concatenate(halves(feat), 0)
     tail = np.zeros((32, 3 * 128), np.float32)
     head = np.zeros((48, 6 * 128), np.float32)
-    place = np.zeros((48, 3 * 128), np.float32)
+    place = np.zeros((48, 18 * 128), np.float32)
     for i in range(3):
         for r in range(8):
             tail[i * 8 + r, i * 128 + 120 + r] = 1
             for h in range(2):
                 head[i * 16 + h * 8 + r, (i * 2 + h) * 128 + r] = 1
-                place[i * 16 + h * 8 + r, i * 128 + r] = 1
+                for j in range(r + 1, TAPS):
+                    place[i * 16 + h * 8 + r, (i * 6 + j - 1) * 128 + 128 + r - j] = 1
     as16 = lambda x: x.astype(ml_dtypes.bfloat16)
-    return (c1_two, c1_three, d1_three, fwd_three, inv_three, twist, feat_hi, feat_lo,
+    return (c1_two, c1_three, d1_three, fwd_three, inv_three, twist, feat_two,
             as16(tail), as16(head), as16(place))
 
 
@@ -107,18 +109,23 @@
 
 
 def kernel(quads, stacks,
-           q_ref, k_ref, v_ref, cot_ref, taps_ref, fin_ref, fout_ref, decay_ref, skip_ref,
-           c1_two, c1_three, d1_three, fwd_three, inv_three, twist, feat_hi, feat_lo,
-           tail_sel, head_sel, head_place,
-           mixed_ref, qg_ref, kg_ref, vg_ref, tg_ref, fig_ref, fog_ref, sg_ref,
-           tails_out, tails_in, heads_out, heads_in, tap_rows, tap_cols, fin_pad,
-           prev, shorts, shifted, grads, ahead, bend, act_hi, act_lo, env,
-           sig, sig_u, spec_h, spec_u, spec_g,
-           ug_out, ug_in, conv_out, conv_in, back_out, back_in, bent_hi, bent_lo,
-           prods, tap_tiles, tap_parts, tap_sums, in_tiles, in_parts, in_mine,
-           in_quad, in_next, in_stack, in_sums, in_flat,
-           halo_s, halo_r, ug_s, ug_r, conv_s, conv_r, back_s, back_r,
-           tp_s, tp_r, ts_s, ts_r, ip_s, ip_r, iq_s, iq_r, iz_s, iz_r, is_s, is_r):
+           *refs):
+    sources, refs = refs[:LOADS], refs[LOADS:]
+    targets, refs = refs[:8], refs[8:]
+    held, refs = refs[:LOADS], refs[LOADS:]
+    done, refs = refs[:8], refs[8:]
+    (q_ref, k_ref, v_ref, cot_ref, taps_ref, fin_ref, fout_ref, decay_ref, skip_ref,
+     c1_two, c1_three, d1_three, fwd_three, inv_three, twist, feat,
+     tail_sel, head_sel, head_place) = held
+    mixed_ref, qg_ref, kg_ref, vg_ref, tg_ref, fig_ref, fog_ref, sg_ref = done
+    (load_s, store_s, tails_out, tails_in, heads_out, heads_in, tap_rows, tap_cols, fin_pad,
+     tap_wide, prev, after, shorts, shifted, grads, ahead, bend, act, env,
+     sig, sig_u, spec_h, spec_u, spec_g,
+     ug_out, ug_in, conv_out, conv_in, back_out, back_in, bent, slope,
+     prods, tap_tiles, tap_parts, tap_sums, in_tiles, in_parts,
+     in_quad, in_stack, in_sums, in_flat,
+     halo_s, halo_r, ug_s, ug_r, conv_s, conv_r, back_s, back_r,
+     tp_s, tp_r, ts_s, ts_r, ip_s, ip_r, iq_s, iq_r, iz_s, iz_r, is_s, is_r) = refs
     me = lax.axis_index("ctx")
     ch = lax.axis_index("chan")
     layer = ch // quads
@@ -136,11 +143,8 @@
             device_id=where, device_id_type=MESH)
 
     def each(count, body, start=1):
-        def step(d, carry):
+        for d in range(start, count):
             body(d)
-            return carry
-        if count > start:
-            lax.fori_loop(start, count, step, 0)
 
     def other(d):
         return lax.rem(me + d, NCTX)
@@ -160,12 +164,24 @@
     each(quads, lambda d: greet(over(quad_peer(d))))
     each(stacks, lambda d: greet(over(stack_peer(d))))
 
+    def load(k):
+        return pltpu.make_async_copy(sources[k], held[k], load_s.at[k])
+
+    def store(k):
+        return pltpu.make_async_copy(done[k], targets[k], store_s.at[k])
+
+    for k in (0, 1, 2, 16, 4, 5, 15, 3, 6, 7, 8, 14, 10, 12, 9, 11, 13, 17, 18):
+        load(k).start()
+
+    for k in (0, 1, 2, 16):
+        load(k).wait()
     ends = jnp.concatenate([r[:, 128:256] for r in (q_ref, k_ref, v_ref)], axis=1)
     tails_out[...] = mm(tail_sel[...], ends, 1, 1).astype(bf16)
     pl.semaphore_wait(barrier, NCTX - 1 + (quads - 1) + (stacks - 1))
     tail_copy = copy(tails_out, tails_in, halo_s.at[0], halo_r.at[0], at(other(1)))
     tail_copy.start()
 
+    load(4).wait()
     tap_rows[...] = jnp.zeros_like(tap_rows)
     for i in range(3):
         tap_rows[i * 8 : i * 8 + TAPS, :] = taps_ref[i]
@@ -175,29 +191,42 @@
     hi, lo = split(tap_rows[...])
     rest = (tap_rows[...] - hi.astype(f32) - lo.astype(f32)).astype(bf16)
     tap_cols[...] = mm(hi, unit, 0, 0) + mm(lo, unit, 0, 0) + mm(rest, unit, 0, 0)
-
+    ROWS = 32
+    CHUNKS = 256 // ROWS
+
+    def spread(d):
+        rows = pl.ds(d * ROWS, ROWS)
+        for i in range(3):
+            for j in range(TAPS):
+                one = tap_cols[rows, i * 8 + j : i * 8 + j + 1]
+                tap_wide[i * TAPS + j, rows, :] = jnp.broadcast_to(one, (ROWS, 128))
+
+    each(CHUNKS, spread, 0)
+
+    load(5).wait()
+    load(15).wait()
     fin_pad[...] = jnp.zeros_like(fin_pad)
     fin_pad[0:EMB, :] = fin_ref[...]
     fin_hi, fin_lo = split(fin_pad[...])
+    fin_three = jnp.concatenate([fin_hi, fin_hi, fin_lo], axis=0)
     WIDE = 512
 
     def network(d):
-        cols = pl.ds(pl.multiple_of(d * WIDE, WIDE), WIDE)
-        a, b = feat_hi[:, cols], feat_lo[:, cols]
-        pre = mm(fin_hi, a, 0, 0) + mm(fin_lo, a, 0, 0) + mm(fin_hi, b, 0, 0)
+        cols = pl.ds(d * WIDE, WIDE)
+        f = feat[:, cols]
+        pre = mm(fin_three, jnp.concatenate([f, f[0:FEAT, :]], axis=0), 0, 0)
         s, c = sin_cos(pre)
         bend[:, cols] = c
         a, b = split(s)
-        act_hi[:, cols] = a
-        act_lo[:, cols] = b
+        act[0:FH, cols] = a
+        act[FH : 2 * FH, cols] = b
 
     each(SEQ // WIDE, network, 0)
 
+    load(3).wait()
     tail_copy.wait_recv()
     inside = jnp.where(me > 0, 1.0, 0.0)
-    prev[...] = mm(tails_in[...], tail_sel[...], 0, 0) * inside
-    ROWS = 32
-    CHUNKS = 256 // ROWS
+    prev[...] = (mm(tails_in[...], tail_sel[...], 0, 0) * inside).astype(bf16)
 
     def moved(x, by):
         return x if by == 0 else pltpu.roll(x, by, 1)
@@ -207,11 +236,13 @@
         rows = pl.ds(pl.multiple_of(part * ROWS, ROWS), ROWS)
         res = []
         for i, ref in enumerate((q_ref, k_ref, v_ref)):
-            x = jnp.concatenate(
-                [prev[rows, i * 128 : (i + 1) * 128], ref[rows, :].astype(f32)], axis=1)
+            x = jnp.concatenate([prev[rows, i * 128 : (i + 1) * 128], ref[rows, :]], axis=1)
             acc = None
             for j in range(TAPS):
-                term = tap_cols[rows, i * 8 + j : i * 8 + j + 1] * moved(x, j)[:, 128:384]
+                y = moved(x, j)[:, 128:384]
+                shifted[i * TAPS + j, rows, :] = y
+                tap = tap_wide[i * TAPS + j, rows, :]
+                term = jnp.concatenate([tap, tap], axis=1) * y.astype(f32)
                 acc = term if acc is None else acc + term
             shorts[i, rows, :] = acc
             res.append(acc)
@@ -221,35 +252,40 @@
             p = part * 2 + h
             ug_out[p, 0:16, :] = u[h * 16 : (h + 1) * 16, :]
             ug_out[p, 16:32, :] = g[h * 16 : (h + 1) * 16, :]
-
-            @pl.when(p != me)
-            def _():
-                copy(ug_out.at[p], ug_in.at[me], ug_s.at[p], ug_r.at[me], at(p)).start()
+        mate = part * 2 + 1 - lax.rem(me, 2)
+        for p in ((mate,) if d == 0 else (part * 2, part * 2 + 1)):
+            copy(ug_out.at[p], ug_in.at[me], ug_s.at[p], ug_r.at[me], at(p)).start()
 
     each(CHUNKS, short_part, 0)
     ug_in[me] = ug_out[me]
 
+    for k in (6, 7, 8):
+        load(k).wait()
     eye = (lax.broadcasted_iota(jnp.int32, (OWN, OWN), 0)
            == lax.broadcasted_iota(jnp.int32, (OWN, OWN), 1)).astype(f32)
     decay = jnp.sum(eye * decay_ref[...], axis=1, keepdims=True)
     skip = jnp.sum(eye * skip_ref[...], axis=1, keepdims=True)
     w_hi, w_lo = split(fout_ref[...])
+    w_two = jnp.concatenate([w_hi, w_lo], axis=0)
+    w_three = jnp.concatenate([w_hi, w_hi, w_lo], axis=0)
     scale = 1.0 / math.sqrt(SEQ)
 
     def filters(d):
-        cols = pl.ds(pl.multiple_of(d * WIDE, WIDE), WIDE)
-        a, b = act_hi[:, cols], act_lo[:, cols]
-        raw = mm(w_hi, a, 0, 0) + mm(w_lo, a, 0, 0) + mm(w_hi, b, 0, 0)
+        cols = pl.ds(d * WIDE, WIDE)
+        raw = mm(w_two, act[0:FH, cols])
+        raw = raw[0:OWN, :] + raw[OWN : 2 * OWN, :] + mm(w_hi, act[FH : 2 * FH, cols])
         t = (d * WIDE + lax.broadcasted_iota(jnp.int32, (OWN, WIDE), 1)).astype(f32)
         e = jnp.exp(-decay * (t * (1.0 / SEQ))) * scale
         h = raw * e
         for n in range(WIDE // 128):
-            rows = pl.ds(pl.multiple_of((d * (WIDE // 128) + n) * OWN, OWN), OWN)
+            rows = pl.ds((d * (WIDE // 128) + n) * OWN, OWN)
             env[rows, :] = e[:, n * 128 : (n + 1) * 128]
             sig[rows, :] = h[:, n * 128 : (n + 1) * 128]
 
     each(SEQ // WIDE, filters, 0)
 
+    for k in (9, 10, 11, 12, 13, 14):
+        load(k).wait()
     GRP = 4
     tc, ts = twist[0:K1, :], twist[K1 : 2 * K1, :]
 
@@ -296,16 +332,6 @@
 
     forward(sig, spec_h, False)
 
-    def shift_part(d):
-        rows = pl.ds(pl.multiple_of(d * ROWS, ROWS), ROWS)
-        for i, ref in enumerate((q_ref, k_ref, v_ref)):
-            x = jnp.concatenate(
-                [prev[rows, i * 128 : (i + 1) * 128], ref[rows, :].astype(f32)], axis=1)
-            for j in range(TAPS):
-                shifted[i * TAPS + j, rows, :] = moved(x, j)[:, 128:384].astype(bf16)
-
-    each(CHUNKS, shift_part, 0)
-
     def ug_wait(d):
         p = other(d)
         copy(ug_out.at[p], ug_in.at[p], ug_s.at[p], ug_r.at[p], at(p)).wait_recv()
@@ -341,28 +367,29 @@
 
     backward(spec_g, spec_u, True, sig)
     sg_ref[...] = jnp.sum(eye * sig[0:16, 0:1], axis=0, keepdims=True) * scale
+    store(7).start()
     for n in range(BLK):
+        cols = slice(n * 128, (n + 1) * 128)
         a, b = split(sig[n * 16 : (n + 1) * 16, :] * env[n * 16 : (n + 1) * 16, :])
-        bent_hi[:, n * 128 : (n + 1) * 128] = a
-        bent_lo[:, n * 128 : (n + 1) * 128] = b
-
-    def gradient(d, carry):
-        out_sum, in_sum = carry
-        cols = pl.ds(pl.multiple_of(d * WIDE, WIDE), WIDE)
-        bh, bl = bent_hi[:, cols], bent_lo[:, cols]
-        ah, al = act_hi[:, cols], act_lo[:, cols]
-        out_sum = out_sum + mm(ah, bh, 1, 1) + mm(al, bh, 1, 1) + mm(ah, bl, 1, 1)
-        slope = (mm(w_hi, bh) + mm(w_lo, bh) + mm(w_hi, bl)) * bend[:, cols]
-        sh, sl = split(slope)
-        fh, fl = feat_hi[:, cols], feat_lo[:, cols]
-        in_sum = in_sum + mm(fh, sh, 1, 1) + mm(fl, sh, 1, 1) + mm(fh, sl, 1, 1)
-        return out_sum, in_sum
-
-    out_sum, in_sum = lax.fori_loop(
-        0, SEQ // WIDE, gradient, (jnp.zeros((FH, OWN), f32), jnp.zeros((FEAT, FH), f32)))
-    fog_ref[...] = out_sum * scale
+        bent[0:16, cols] = a
+        bent[16:32, cols] = b
+        bent[32:48, cols] = a
+    total = mm(bent[0:32, :], act[...], 1, 1)
+    fog_ref[...] = (total[0:OWN, 0:FH] + total[OWN : 2 * OWN, 0:FH]
+                    + pltpu.roll(total[0:OWN, :], FH, 1)[:, 0:FH]) * scale
+    store(6).start()
+
+    def slopes(d):
+        cols = pl.ds(d * 2 * WIDE, 2 * WIDE)
+        a, b = split(mm(w_three, bent[:, cols], 0, 0) * bend[:, cols])
+        slope[0:FH, cols] = a
+        slope[FH : 2 * FH, cols] = b
+
+    each(SEQ // (2 * WIDE), slopes, 0)
+    total = mm(feat[...], slope[...], 1, 1)
+    in_sum = (total[0:FEAT, :] + total[FEAT : 2 * FEAT, :] + pltpu.roll(total[0:FEAT, :], FH, 1))
     in_flat[...] = jnp.zeros_like(in_flat)
-    in_flat[:, 0:FH] = in_sum
+    in_flat[:, 0:FH] = in_sum[:, 0:FH]
     packed = in_flat[0:24, :] + pltpu.roll(in_flat[24:48, :], 64, 1)
     for k in range(3):
         in_tiles[k] = packed[k * 8 : (k + 1) * 8, :]
@@ -391,7 +418,7 @@
     rows_wait(back_out, back_in, back_s, back_r)
 
     def grad_part(d):
-        rows = pl.ds(pl.multiple_of(d * ROWS, ROWS), ROWS)
+        rows = pl.ds(d * ROWS, ROWS)
         cv = conv_in[rows, :].astype(f32)
         bk = back_in[rows, :].astype(f32)
         mixed_ref[rows, :] = (shorts[0, rows, :] * cv).astype(bf16)
@@ -403,6 +430,9 @@
             ahead[rows, i * 256 + 128 : i * 256 + 256] = lo
 
     each(CHUNKS, grad_part, 0)
+    store(0).start()
+    load(17).wait()
+    load(18).wait()
     heads_out[...] = mm(head_sel[...], ahead[...], 1, 1).astype(bf16)
     head_copy = copy(heads_out, heads_in, halo_s.at[1], halo_r.at[1], at(other(NCTX - 1)))
     head_copy.start()
@@ -429,7 +459,7 @@
         each(quads, go)
 
     def prod_part(d):
-        rows = pl.ds(pl.multiple_of(d * ROWS, ROWS), ROWS)
+        rows = pl.ds(d * ROWS, ROWS)
         for i in range(3):
             g = grads[i, rows, :]
             for j in range(TAPS):
@@ -467,20 +497,30 @@
 
     head_copy.wait_recv()
     before_end = jnp.where(me < NCTX - 1, 1.0, 0.0)
-    prev[...] = mm(heads_in[...], head_place[...], 0, 0) * before_end
-
-    def proj_part(d):
-        rows = pl.ds(pl.multiple_of(d * ROWS, ROWS), ROWS)
-        for i, ref in enumerate((qg_ref, kg_ref, vg_ref)):
-            x = jnp.concatenate([grads[i, rows, :], prev[rows, i * 128 : (i + 1) * 128]], axis=1)
-            acc = None
-            for j in range(TAPS):
-                y = moved(x, (384 - j) % 384)[:, 0:256]
-                term = tap_cols[rows, i * 8 + j : i * 8 + j + 1] * y
-                acc = term if acc is None else acc + term
-            ref[rows, :] = acc.astype(bf16)
-
-    each(CHUNKS, proj_part, 0)
+    after[...] = mm(heads_in[...], head_place[...], 0, 0) * before_end
+    lane = lax.broadcasted_iota(jnp.int32, (ROWS, 128), 1)
+
+    def proj(i, ref):
+        def proj_part(d):
+            rows = slice(d * ROWS, (d + 1) * ROWS)
+            left, right = grads[i, rows, 0:128], grads[i, rows, 128:256]
+            tap = tap_wide[i * TAPS, rows, :]
+            acc = [tap * left, tap * right]
+            for j in range(1, TAPS):
+                tap = tap_wide[i * TAPS + j, rows, :]
+                near, far = pltpu.roll(left, 128 - j, 1), pltpu.roll(right, 128 - j, 1)
+                edge = after[rows, (i * 6 + j - 1) * 128 : (i * 6 + j) * 128]
+                here = lane < 128 - j
+                acc[0] = acc[0] + tap * jnp.where(here, near, far)
+                acc[1] = acc[1] + tap * jnp.where(here, far, edge)
+            ref[rows, 0:128] = acc[0].astype(bf16)
+            ref[rows, 128:256] = acc[1].astype(bf16)
+
+        for d in range(CHUNKS):
+            proj_part(d)
+        store(1 + i).start()
+
+    proj(0, qg_ref)
 
     @pl.when(tap_owner)
     def _():
@@ -507,6 +547,9 @@
                  at(other(d))).start()
         each(NCTX, go)
 
+    proj(1, kg_ref)
+    proj(2, vg_ref)
+
     for k in range(6):
         @pl.when(me != 2 * k)
         def _(k=k):
@@ -514,6 +557,7 @@
     for i in range(3):
         both = jnp.concatenate([tap_sums[2 * i], tap_sums[2 * i + 1]], axis=1) * scale
         tg_ref[i] = both[0:TAPS, :]
+    store(4).start()
     for k in range(3):
         @pl.when(me != 2 * k + 1)
         def _(k=k):
@@ -521,7 +565,10 @@
     sums = jnp.concatenate([in_sums[k] for k in range(3)], axis=0) * (scale / math.sqrt(D))
     fig_ref[0:24, :] = sums[:, 0:FH]
     fig_ref[24:EMB, :] = pltpu.roll(sums, 64, 1)[0 : EMB - 24, 0:FH]
-
+    store(5).start()
+
+    for k in range(8):
+        store(k).wait()
     tail_copy.wait_send()
     head_copy.wait_send()
     deal(3, 1, in_tiles, in_parts, ip_s, ip_r, lambda c: c.wait_send())
@@ -551,41 +598,58 @@
                                   ts_r.at[tap_index], at(other(d))).wait_send())
 
 
+def hand_on(*refs):
+    held, load_s, store_s = refs[16:24], refs[24], refs[25]
+    loads = [pltpu.make_async_copy(refs[k], held[k], load_s.at[k]) for k in range(8)]
+    stores = [pltpu.make_async_copy(held[k], refs[8 + k], store_s.at[k]) for k in range(8)]
+    for c in loads:
+        c.start()
+    for k in range(8):
+        loads[k].wait()
+        stores[k].start()
+    for c in stores:
+        c.wait()
+
+
 def per_device(consts, chans, query_proj, key_proj, value_proj, out_cotangent, short_taps,
                filter_in, filter_out, decay_rate, skip_gain):
     quads = math.gcd(chans, 4)
     stacks = chans // quads
-    vm = pl.BlockSpec(memory_space=pltpu.VMEM)
     block = jax.ShapeDtypeStruct((256, POS), bf16)
     dma = pltpu.SemaphoreType.DMA
     V = pltpu.VMEM
-    args = (query_proj, key_proj, value_proj, out_cotangent, short_taps, filter_in, filter_out,
-            decay_rate.reshape(1, OWN), skip_gain.reshape(1, OWN))
+    args = [query_proj, key_proj, value_proj, out_cotangent, short_taps, filter_in, filter_out.T,
+            decay_rate.reshape(1, OWN), skip_gain.reshape(1, OWN)]
+    args += [jnp.asarray(c) for c in consts]
+    shapes = (block, block, block, block,
+              jax.ShapeDtypeStruct((3, TAPS, 256), f32),
+              jax.ShapeDtypeStruct((EMB, FH), f32),
+              jax.ShapeDtypeStruct((OWN, FH), f32),
+              jax.ShapeDtypeStruct((1, OWN), f32))
+    hbm = pl.BlockSpec(memory_space=pl.ANY)
     outs = pl.pallas_call(
         functools.partial(kernel, quads, stacks),
-        out_shape=(block, block, block, block,
-                   jax.ShapeDtypeStruct((3, TAPS, 256), f32),
-                   jax.ShapeDtypeStruct((EMB, FH), f32),
-                   jax.ShapeDtypeStruct((FH, OWN), f32),
-                   jax.ShapeDtypeStruct((1, OWN), f32)),
-        in_specs=[vm] * (len(args) + len(consts)),
-        out_specs=[vm] * 8,
-        scratch_shapes=[
+        out_shape=shapes,
+        in_specs=[hbm] * LOADS,
+        out_specs=[hbm] * 8,
+        scratch_shapes=[V(a.shape, a.dtype) for a in args] + [V(a.shape, a.dtype) for a in shapes] + [
+            dma((LOADS,)), dma((8,)),
             V((32, 256), bf16), V((32, 256), bf16), V((48, 256), bf16), V((48, 256), bf16),
             V((24, 256), f32), V((256, 128), f32), V((FEAT, FH), f32),
-            V((256, 384), f32), V((3, 256, 256), f32), V((21, 256, 256), bf16),
+            V((21, 256, 128), f32), V((256, 384), bf16), V((256, 18 * 128), f32),
+            V((3, 256, 256), f32), V((21, 256, 256), bf16),
             V((3, 256, 256), f32), V((256, 768), bf16), V((FH, SEQ), f32),
-            V((FH, SEQ), bf16), V((FH, SEQ), bf16), V((512, 128), f32),
+            V((2 * FH, SEQ), bf16), V((512, 128), f32),
             V((512, 128), f32), V((512, 128), f32),
             V((OWN * K1, 256), f32), V((OWN * K1, 256), f32), V((OWN * K1, 256), f32),
             V((NCTX, 32, 256), bf16), V((NCTX, 32, 256), bf16),
             V((NCTX, 16, 256), bf16), V((256, 256), bf16),
             V((NCTX, 16, 256), bf16), V((256, 256), bf16),
-            V((OWN, SEQ), bf16), V((OWN, SEQ), bf16),
+            V((3 * OWN, SEQ), bf16), V((2 * FH, SEQ), bf16),
             V((21, 256, 256), bf16), V((6, 8, 128), f32), V((NCTX, 8, 128), f32),
             V((6, 8, 128), f32),
-            V((3, 8, 128), f32), V((NCTX, 8, 128), f32), V((8, 128), f32),
-            V((quads, 8, 128), f32), V((8, 128), f32), V((stacks, 8, 128), f32),
+            V((3, 8, 128), f32), V((NCTX, 8, 128), f32),
+            V((quads, 8, 128), f32), V((stacks, 8, 128), f32),
             V((3, 8, 128), f32), V((48, 128), f32),
             dma((2,)), dma((2,)), dma((NCTX,)), dma((NCTX,)),
             dma((NCTX,)), dma((NCTX,)), dma((NCTX,)), dma((NCTX,)),
@@ -595,8 +659,15 @@
         ],
         compiler_params=pltpu.CompilerParams(
             collective_id=0, has_side_effects=True, vmem_limit_bytes=56 * 1024 * 1024),
-    )(*args, *[jnp.asarray(c) for c in consts])
-    return outs[:7] + (outs[7].reshape(OWN),)
+    )(*args)
+    outs = pl.pallas_call(
+        hand_on,
+        out_shape=shapes,
+        in_specs=[hbm] * 8,
+        out_specs=[hbm] * 8,
+        scratch_shapes=[V(a.shape, a.dtype) for a in shapes] + [dma((8,)), dma((8,))],
+    )(*outs)
+    return outs[:6] + (outs[6].T, outs[7].reshape(OWN))
 
 
 def solution(mesh):

time: 69.2 us -> 55.4 us (0.80)
  local copies, waits for them, and re-layouts: 8.92 us -> 0 us
  Pallas kernels: 59.1 us -> 54.6 us
    unnamed x21 -> x0, local copies, waits for them, and re-layouts: 8.92 us -> none
    pallas_call x1 -> x2, Pallas kernels: 59.1 us -> 54.6 us  [the longest x1 52.7 us: per_device(): pl.pallas_call(functools.partial(kernel, quads, stacks), out_shape=shapes...]
where the time goes in v2:
time: 55.4 us; the launch traced here: 55.3 us
  Pallas kernels  54.6 us (99%)
  between operations  0.64 us (1%)
    pallas_call x1, Pallas kernels, per_device(): pl.pallas_call(functools.partial(kernel, quads, stacks), out_shape=shapes...  52.7 us
    pallas_call x1, Pallas kernels, per_device(): pl.pallas_call(hand_on, out_shape=shapes, in_specs=[hbm] * 8, out_specs=[...  1.9 us

profile of v2, /device:TPU:2, one launch (start us, length us, event | category | flops | bytes accessed | tf_op | source)
XLA Modules:
  0.0 55.3 jit_solution(9076008993486804351)
XLA Ops:
  0.6 52.7 %shard_map.242 = (bf16[256,256]{1,0:T(8,128)(2,1)}, bf16[256,256]{1,0:T(8,128)(2,1)}, bf16[256,256]{1,0:T(8,128)(2,1)}, bf16[256,256]{1,0:T(8,128)(2,1)}, f32[3,...) custom-call(bf16[256,256]{1,0:T(8,128)(2,1)} %refs_0_.1, bf16[256,256]{1,0:T(8,128)(2,1)} %refs_1_.1, ...), custom_call_target="tpu_custom_call" | custom-call | tf_op jit(solution)/shard_map/pallas_call | solution.py:630
  53.4 1.9 %shard_map.243 = (bf16[256,256]{1,0:T(8,128)(2,1)}, bf16[256,256]{1,0:T(8,128)(2,1)}, bf16[256,256]{1,0:T(8,128)(2,1)}, bf16[256,256]{1,0:T(8,128)(2,1)}, f32[3,...) custom-call(bf16[256,256]{1,0:T(8,128)(2,1)} %get-tuple-element.24.refs_0_, ...), custom_call_target="tpu_custom_call" | custom-call | tf_op jit(solution)/shard_map/pallas_call | solution.py:663

commit v3 on v2

--- a/solution.py
+++ b/solution.py
@@ -24,6 +24,9 @@
 BLK = SEQ // N2
 FEAT = 48
 LOADS = 19
+YS = 8
+STEPS = sorted(((dx, dy) for dx in range(2) for dy in range(YS) if dx + dy > 0),
+               key=lambda s: (-s[0] - min(s[1], YS - s[1]), s))
 MESH = pl.DeviceIdType.MESH
 f32 = jnp.float32
 bf16 = jnp.bfloat16
@@ -108,7 +111,7 @@
     return s * r * sign, c * sign
 
 
-def kernel(quads, stacks,
+def kernel(chans,
            *refs):
     sources, refs = refs[:LOADS], refs[LOADS:]
     targets, refs = refs[:8], refs[8:]
@@ -121,15 +124,12 @@
     (load_s, store_s, tails_out, tails_in, heads_out, heads_in, tap_rows, tap_cols, fin_pad,
      tap_wide, prev, after, shorts, shifted, grads, ahead, bend, act, env,
      sig, sig_u, spec_h, spec_u, spec_g,
-     ug_out, ug_in, conv_out, conv_in, back_out, back_in, bent, slope,
-     prods, tap_tiles, tap_parts, tap_sums, in_tiles, in_parts,
-     in_quad, in_stack, in_sums, in_flat,
-     halo_s, halo_r, ug_s, ug_r, conv_s, conv_r, back_s, back_r,
-     tp_s, tp_r, ts_s, ts_r, ip_s, ip_r, iq_s, iq_r, iz_s, iz_r, is_s, is_r) = refs
+     u_out, u_in, g_out, g_in, conv_out, conv_in, back_out, back_in, bent, slope,
+     prods, tap_out, tap_in, in_tiles, in_parts, in_row, in_sums, in_flat,
+     halo_s, halo_r, u_s, u_r, g_s, g_r, conv_s, conv_r, back_s, back_r,
+     tp_s, tp_r, ip_s, ip_r, iq_s, iq_r, is_s, is_r) = refs
     me = lax.axis_index("ctx")
     ch = lax.axis_index("chan")
-    layer = ch // quads
-    member = ch % quads
 
     def at(ctx_index):
         return {"ctx": ctx_index, "chan": ch}
@@ -149,20 +149,26 @@
     def other(d):
         return lax.rem(me + d, NCTX)
 
-    def quad_peer(d):
-        return layer * quads + lax.rem(member + d, quads)
-
-    def stack_peer(d):
-        return lax.rem(layer + d, stacks) * quads + member
+    def peers(body):
+        for dx, dy in STEPS:
+            body(lax.rem(me // YS + dx, NCTX // YS) * YS + lax.rem(me % YS + dy, YS))
+
+    def chan_peer(d):
+        return lax.rem(ch + d, chans)
+
+    in_owner = jnp.logical_and(lax.rem(me, 2) == 1, me < 6)
+    in_index = jnp.minimum(me // 2, 2)
 
     barrier = pltpu.get_barrier_semaphore()
 
     def greet(where):
         pl.semaphore_signal(barrier, inc=1, device_id=where, device_id_type=MESH)
 
-    each(NCTX, lambda d: greet(at(other(d))))
-    each(quads, lambda d: greet(over(quad_peer(d))))
-    each(stacks, lambda d: greet(over(stack_peer(d))))
+    peers(lambda p: greet(at(p)))
+
+    @pl.when(in_owner)
+    def _():
+        each(chans, lambda d: greet(over(chan_peer(d))))
 
     def load(k):
         return pltpu.make_async_copy(sources[k], held[k], load_s.at[k])
@@ -177,7 +183,7 @@
         load(k).wait()
     ends = jnp.concatenate([r[:, 128:256] for r in (q_ref, k_ref, v_ref)], axis=1)
     tails_out[...] = mm(tail_sel[...], ends, 1, 1).astype(bf16)
-    pl.semaphore_wait(barrier, NCTX - 1 + (quads - 1) + (stacks - 1))
+    pl.semaphore_wait(barrier, jnp.where(in_owner, NCTX - 1 + chans - 1, NCTX - 1))
     tail_copy = copy(tails_out, tails_in, halo_s.at[0], halo_r.at[0], at(other(1)))
     tail_copy.start()
 
@@ -223,7 +229,6 @@
 
     each(SEQ // WIDE, network, 0)
 
-    load(3).wait()
     tail_copy.wait_recv()
     inside = jnp.where(me > 0, 1.0, 0.0)
     prev[...] = (mm(tails_in[...], tail_sel[...], 0, 0) * inside).astype(bf16)
@@ -231,33 +236,37 @@
     def moved(x, by):
         return x if by == 0 else pltpu.roll(x, by, 1)
 
-    def short_part(d):
-        part = lax.rem(me // 2 + d, CHUNKS)
-        rows = pl.ds(pl.multiple_of(part * ROWS, ROWS), ROWS)
-        res = []
-        for i, ref in enumerate((q_ref, k_ref, v_ref)):
-            x = jnp.concatenate([prev[rows, i * 128 : (i + 1) * 128], ref[rows, :]], axis=1)
-            acc = None
-            for j in range(TAPS):
-                y = moved(x, j)[:, 128:384]
-                shifted[i * TAPS + j, rows, :] = y
-                tap = tap_wide[i * TAPS + j, rows, :]
-                term = jnp.concatenate([tap, tap], axis=1) * y.astype(f32)
-                acc = term if acc is None else acc + term
-            shorts[i, rows, :] = acc
-            res.append(acc)
-        u = (res[1] * res[2]).astype(bf16)
-        g = (cot_ref[rows, :].astype(f32) * res[0]).astype(bf16)
-        for h in range(2):
-            p = part * 2 + h
-            ug_out[p, 0:16, :] = u[h * 16 : (h + 1) * 16, :]
-            ug_out[p, 16:32, :] = g[h * 16 : (h + 1) * 16, :]
-        mate = part * 2 + 1 - lax.rem(me, 2)
-        for p in ((mate,) if d == 0 else (part * 2, part * 2 + 1)):
-            copy(ug_out.at[p], ug_in.at[me], ug_s.at[p], ug_r.at[me], at(p)).start()
-
-    each(CHUNKS, short_part, 0)
-    ug_in[me] = ug_out[me]
+    def short(i, ref, rows):
+        x = jnp.concatenate([prev[rows, i * 128 : (i + 1) * 128], ref[rows, :]], axis=1)
+        acc = None
+        for j in range(TAPS):
+            y = moved(x, j)[:, 128:384]
+            shifted[i * TAPS + j, rows, :] = y
+            tap = tap_wide[i * TAPS + j, rows, :]
+            term = jnp.concatenate([tap, tap], axis=1) * y.astype(f32)
+            acc = term if acc is None else acc + term
+        shorts[i, rows, :] = acc
+        return acc
+
+    def scatter(out, inn, send, recv):
+        inn[me] = out[me]
+        peers(lambda p: copy(out.at[p], inn.at[me], send.at[p], recv.at[me], at(p)).start())
+
+    def short_part(which, out):
+        for part in range(CHUNKS):
+            rows = pl.ds(part * ROWS, ROWS)
+            if which == 0:
+                x = short(1, k_ref, rows) * short(2, v_ref, rows)
+            else:
+                x = cot_ref[rows, :].astype(f32) * short(0, q_ref, rows)
+            for h in range(2):
+                out[part * 2 + h] = x[h * 16 : (h + 1) * 16, :].astype(bf16)
+
+    short_part(0, u_out)
+    scatter(u_out, u_in, u_s, u_r)
+    load(3).wait()
+    short_part(1, g_out)
+    scatter(g_out, g_in, g_s, g_r)
 
     for k in (6, 7, 8):
         load(k).wait()
@@ -332,38 +341,29 @@
 
     forward(sig, spec_h, False)
 
-    def ug_wait(d):
-        p = other(d)
-        copy(ug_out.at[p], ug_in.at[p], ug_s.at[p], ug_r.at[p], at(p)).wait_recv()
-
-    each(NCTX, ug_wait)
-    for s in range(NCTX):
-        for h in range(2):
-            n = 2 * s + h
-            sig_u[n * 16 : (n + 1) * 16, :] = ug_in[s, 0:16, h * 128 : (h + 1) * 128].astype(f32)
-            sig[n * 16 : (n + 1) * 16, :] = ug_in[s, 16:32, h * 128 : (h + 1) * 128].astype(f32)
-    forward(sig_u, spec_u, True)
-    forward(sig, spec_g, True)
-
-    def scatter(result, first_row, out, inn, send, recv):
+    def wait_all(out, inn, send, recv):
+        peers(lambda p: copy(out.at[p], inn.at[p], send.at[p], recv.at[p], at(p)).wait_recv())
+
+    def unfold(inn, dst):
+        for n in range(BLK):
+            half = n % 2 * 128
+            dst[n * 16 : (n + 1) * 16, :] = inn[n // 2, :, half : half + 128].astype(f32)
+
+    def fold(result, direct, out):
         for s in range(NCTX):
             x = jnp.concatenate(
                 [result[(2 * s + h) * 16 : (2 * s + h + 1) * 16, :] for h in range(2)], axis=1)
-            x = x + skip * ug_in[s, first_row : first_row + 16, :].astype(f32)
-            out[s] = x.astype(bf16)
-        mine = pl.ds(pl.multiple_of(me * 16, 16), 16)
-        inn[mine, :] = out[me]
-
-        def go(d):
-            p = other(d)
-            copy(out.at[p], inn.at[mine, :], send.at[p], recv.at[me], at(p)).start()
-
-        each(NCTX, go)
-
+            out[s] = (x + skip * direct[s].astype(f32)).astype(bf16)
+
+    wait_all(u_out, u_in, u_s, u_r)
+    unfold(u_in, sig_u)
+    forward(sig_u, spec_u, True)
     backward(spec_u, spec_h, False, sig_u)
-    scatter(sig_u, 0, conv_out, conv_in, conv_s, conv_r)
-    backward(spec_g, spec_h, True, sig)
-    scatter(sig, 16, back_out, back_in, back_s, back_r)
+    fold(sig_u, u_in, conv_out)
+    scatter(conv_out, conv_in, conv_s, conv_r)
+    wait_all(g_out, g_in, g_s, g_r)
+    unfold(g_in, sig)
+    forward(sig, spec_g, True)
 
     backward(spec_g, spec_u, True, sig)
     sg_ref[...] = jnp.sum(eye * sig[0:16, 0:1], axis=0, keepdims=True) * scale
@@ -374,11 +374,6 @@
         bent[0:16, cols] = a
         bent[16:32, cols] = b
         bent[32:48, cols] = a
-    total = mm(bent[0:32, :], act[...], 1, 1)
-    fog_ref[...] = (total[0:OWN, 0:FH] + total[OWN : 2 * OWN, 0:FH]
-                    + pltpu.roll(total[0:OWN, :], FH, 1)[:, 0:FH]) * scale
-    store(6).start()
-
     def slopes(d):
         cols = pl.ds(d * 2 * WIDE, 2 * WIDE)
         a, b = split(mm(w_three, bent[:, cols], 0, 0) * bend[:, cols])
@@ -394,106 +389,82 @@
     for k in range(3):
         in_tiles[k] = packed[k * 8 : (k + 1) * 8, :]
 
-    def deal(count, odd, tiles, parts, send, recv, go):
-        for k in range(count):
-            @pl.when(me != 2 * k + odd)
+    def deal(go):
+        for k in range(3):
+            @pl.when(me != 2 * k + 1)
             def _(k=k):
-                c = copy(tiles.at[k], parts.at[me], send.at[k], recv.at[me], at(2 * k + odd))
-                go(c)
-
-    deal(3, 1, in_tiles, in_parts, ip_s, ip_r, lambda c: c.start())
-    in_owner = jnp.logical_and(lax.rem(me, 2) == 1, me < 6)
-    tap_owner = jnp.logical_and(lax.rem(me, 2) == 0, me < 12)
-    in_index = jnp.minimum(me // 2, 2)
-    tap_index = jnp.minimum(me // 2, 5)
-
-    def rows_wait(out, inn, send, recv):
-        def one(d):
-            p = other(d)
-            rows = pl.ds(pl.multiple_of(p * 16, 16), 16)
-            copy(out.at[p], inn.at[rows, :], send.at[p], recv.at[p], at(p)).wait_recv()
-        each(NCTX, one)
-
-    rows_wait(conv_out, conv_in, conv_s, conv_r)
-    rows_wait(back_out, back_in, back_s, back_r)
-
-    def grad_part(d):
+                go(copy(in_tiles.at[k], in_parts.at[me], ip_s.at[k], ip_r.at[me], at(2 * k + 1)))
+
+    deal(lambda c: c.start())
+    backward(spec_g, spec_h, True, sig)
+    fold(sig, g_in, back_out)
+    scatter(back_out, back_in, back_s, back_r)
+    total = mm(bent[0:32, :], act[...], 1, 1)
+    fog_ref[...] = (total[0:OWN, 0:FH] + total[OWN : 2 * OWN, 0:FH]
+                    + pltpu.roll(total[0:OWN, :], FH, 1)[:, 0:FH]) * scale
+    store(6).start()
+
+    def take(i, g, rows):
+        grads[i, rows, :] = g
+        hi, lo = split(g[:, 0:128])
+        ahead[rows, i * 256 : i * 256 + 128] = hi
+        ahead[rows, i * 256 + 128 : i * 256 + 256] = lo
+        for j in range(TAPS):
+            x = g * shifted[i * TAPS + j, rows, :].astype(f32)
+            hi, lo = split(x[:, 0:128] + x[:, 128:256])
+            prods[i * TAPS + j, rows, 0:128] = hi
+            prods[i * TAPS + j, rows, 128:256] = lo
+
+    pick_row = lax.broadcasted_iota(jnp.int32, (16, 256), 0)
+
+    def tap_sum(k, which):
+        total = jnp.zeros((16, 256), f32)
+        for n, i in enumerate(which):
+            for j in range(TAPS):
+                pick = (pick_row == n * 8 + j).astype(f32).astype(bf16)
+                total = total + mm(pick, prods[i * TAPS + j], 1, 1)
+        tap_out[k] = total.astype(bf16)
+        tap_in[k, me] = tap_out[k]
+        peers(lambda p: copy(tap_out.at[k], tap_in.at[k, me], tp_s.at[k, p], tp_r.at[k, me],
+                             at(p)).start())
+
+    def conv_part(d):
         rows = pl.ds(d * ROWS, ROWS)
-        cv = conv_in[rows, :].astype(f32)
-        bk = back_in[rows, :].astype(f32)
+        cv = jnp.concatenate([conv_in[2 * d], conv_in[2 * d + 1]], axis=0).astype(f32)
         mixed_ref[rows, :] = (shorts[0, rows, :] * cv).astype(bf16)
-        gs = (cot_ref[rows, :].astype(f32) * cv, bk * shorts[2, rows, :], bk * shorts[1, rows, :])
-        for i in range(3):
-            grads[i, rows, :] = gs[i]
-            hi, lo = split(gs[i][:, 0:128])
-            ahead[rows, i * 256 : i * 256 + 128] = hi
-            ahead[rows, i * 256 + 128 : i * 256 + 256] = lo
-
-    each(CHUNKS, grad_part, 0)
+        take(0, cot_ref[rows, :].astype(f32) * cv, rows)
+
+    def back_part(d):
+        rows = pl.ds(d * ROWS, ROWS)
+        bk = jnp.concatenate([back_in[2 * d], back_in[2 * d + 1]], axis=0).astype(f32)
+        take(1, bk * shorts[2, rows, :], rows)
+        take(2, bk * shorts[1, rows, :], rows)
+
+    wait_all(conv_out, conv_in, conv_s, conv_r)
+    each(CHUNKS, conv_part, 0)
     store(0).start()
+    tap_sum(0, (0,))
+
+    @pl.when(in_owner)
+    def _():
+        peers(lambda p: copy(in_tiles.at[0], in_parts.at[p], ip_r.at[p], ip_r.at[p],
+                             at(p)).wait_recv())
+        in_parts[me] = in_tiles[in_index]
+        t = in_parts[0]
+        for p in range(1, NCTX):
+            t = t + in_parts[p]
+        in_row[ch] = t
+        each(chans, lambda d: copy(in_row.at[ch], in_row.at[ch], iq_s.at[d], iq_r.at[ch],
+                                   over(chan_peer(d))).start())
+
     load(17).wait()
     load(18).wait()
+    wait_all(back_out, back_in, back_s, back_r)
+    each(CHUNKS, back_part, 0)
     heads_out[...] = mm(head_sel[...], ahead[...], 1, 1).astype(bf16)
     head_copy = copy(heads_out, heads_in, halo_s.at[1], halo_r.at[1], at(other(NCTX - 1)))
     head_copy.start()
-
-    def collect(parts, tiles, index, recv, sender_count):
-        def one(d):
-            p = other(d)
-            copy(tiles.at[0], parts.at[p], recv.at[p], recv.at[p], at(p)).wait_recv()
-        each(NCTX, one)
-        parts[me] = tiles[index]
-        total = parts[0]
-        for p in range(1, sender_count):
-            total = total + parts[p]
-        return total
-
-    @pl.when(in_owner)
-    def _():
-        in_quad[member] = collect(in_parts, in_tiles, in_index, ip_r, NCTX)
-
-        def go(d):
-            p = quad_peer(d)
-            copy(in_quad.at[member], in_quad.at[member], iq_s.at[d], iq_r.at[member],
-                 over(p)).start()
-        each(quads, go)
-
-    def prod_part(d):
-        rows = pl.ds(d * ROWS, ROWS)
-        for i in range(3):
-            g = grads[i, rows, :]
-            for j in range(TAPS):
-                x = g * shifted[i * TAPS + j, rows, :].astype(f32)
-                hi, lo = split(x[:, 0:128] + x[:, 128:256])
-                prods[i * TAPS + j, rows, 0:128] = hi
-                prods[i * TAPS + j, rows, 128:256] = lo
-
-    each(CHUNKS, prod_part, 0)
-    pick_row = lax.broadcasted_iota(jnp.int32, (32, 256), 0)
-    total = jnp.zeros((32, 256), f32)
-    for i in range(3):
-        for j in range(TAPS):
-            pick = (pick_row == i * 8 + j).astype(f32).astype(bf16)
-            total = total + mm(pick, prods[i * TAPS + j], 1, 1)
-    for k in range(6):
-        tap_tiles[k] = total[(k // 2) * 8 : (k // 2) * 8 + 8, (k % 2) * 128 : (k % 2) * 128 + 128]
-    deal(6, 0, tap_tiles, tap_parts, tp_s, tp_r, lambda c: c.start())
-
-    @pl.when(in_owner)
-    def _():
-        def one(d):
-            p = lax.rem(member + d, quads)
-            copy(in_quad.at[p], in_quad.at[p], iq_s.at[d], iq_r.at[p], over(quad_peer(d))).wait_recv()
-        each(quads, one)
-        t = in_quad[0]
-        for p in range(1, quads):
-            t = t + in_quad[p]
-        in_stack[layer] = t
-
-        def go(d):
-            copy(in_stack.at[layer], in_stack.at[layer], iz_s.at[d], iz_r.at[layer],
-                 over(stack_peer(d))).start()
-        each(stacks, go)
+    tap_sum(1, (1, 2))
 
     head_copy.wait_recv()
     before_end = jnp.where(me < NCTX - 1, 1.0, 0.0)
@@ -521,42 +492,33 @@
         store(1 + i).start()
 
     proj(0, qg_ref)
-
-    @pl.when(tap_owner)
-    def _():
-        tap_sums[tap_index] = collect(tap_parts, tap_tiles, tap_index, tp_r, NCTX)
-
-        def go(d):
-            copy(tap_sums.at[tap_index], tap_sums.at[tap_index], ts_s.at[d], ts_r.at[tap_index],
-                 at(other(d))).start()
-        each(NCTX, go)
+    proj(1, kg_ref)
+    proj(2, vg_ref)
 
     @pl.when(in_owner)
     def _():
         def one(d):
-            p = lax.rem(layer + d, stacks)
-            copy(in_stack.at[p], in_stack.at[p], iz_s.at[d], iz_r.at[p], over(stack_peer(d))).wait_recv()
-        each(stacks, one)
-        t = in_stack[0]
-        for p in range(1, stacks):
-            t = t + in_stack[p]
+            p = chan_peer(d)
+            copy(in_row.at[p], in_row.at[p], iq_s.at[d], iq_r.at[p], over(p)).wait_recv()
+        each(chans, one)
+        t = in_row[0]
+        for p in range(1, chans):
+            t = t + in_row[p]
         in_sums[in_index] = t
-
-        def go(d):
-            copy(in_sums.at[in_index], in_sums.at[in_index], is_s.at[d], is_r.at[in_index],
-                 at(other(d))).start()
-        each(NCTX, go)
-
-    proj(1, kg_ref)
-    proj(2, vg_ref)
-
-    for k in range(6):
-        @pl.when(me != 2 * k)
-        def _(k=k):
-            copy(tap_sums.at[k], tap_sums.at[k], ts_s.at[0], ts_r.at[k], at(2 * k)).wait_recv()
-    for i in range(3):
-        both = jnp.concatenate([tap_sums[2 * i], tap_sums[2 * i + 1]], axis=1) * scale
-        tg_ref[i] = both[0:TAPS, :]
+        peers(lambda p: copy(in_sums.at[in_index], in_sums.at[in_index], is_s.at[p],
+                             is_r.at[in_index], at(p)).start())
+
+    for k in range(2):
+        peers(lambda p: copy(tap_out.at[k], tap_in.at[k, p], tp_s.at[k, p], tp_r.at[k, p],
+                             at(p)).wait_recv())
+        t = tap_in[k, 0].astype(f32)
+        for p in range(1, NCTX):
+            t = t + tap_in[k, p].astype(f32)
+        if k == 0:
+            tg_ref[0] = t[0:TAPS, :] * scale
+        else:
+            tg_ref[1] = t[0:TAPS, :] * scale
+            tg_ref[2] = t[8 : 8 + TAPS, :] * scale
     store(4).start()
     for k in range(3):
         @pl.when(me != 2 * k + 1)
@@ -571,31 +533,24 @@
         store(k).wait()
     tail_copy.wait_send()
     head_copy.wait_send()
-    deal(3, 1, in_tiles, in_parts, ip_s, ip_r, lambda c: c.wait_send())
-    deal(6, 0, tap_tiles, tap_parts, tp_s, tp_r, lambda c: c.wait_send())
-
-    def left(d):
-        p = other(d)
-        mine = pl.ds(pl.multiple_of(me * 16, 16), 16)
-        copy(ug_out.at[p], ug_in.at[me], ug_s.at[p], ug_r.at[me], at(p)).wait_send()
-        copy(conv_out.at[p], conv_in.at[mine, :], conv_s.at[p], conv_r.at[me], at(p)).wait_send()
-        copy(back_out.at[p], back_in.at[mine, :], back_s.at[p], back_r.at[me], at(p)).wait_send()
-
-    each(NCTX, left)
+    deal(lambda c: c.wait_send())
+
+    def left(p):
+        for out, inn, send, recv in ((u_out, u_in, u_s, u_r), (g_out, g_in, g_s, g_r),
+                                     (conv_out, conv_in, conv_s, conv_r),
+                                     (back_out, back_in, back_s, back_r)):
+            copy(out.at[p], inn.at[me], send.at[p], recv.at[me], at(p)).wait_send()
+        for k in range(2):
+            copy(tap_out.at[k], tap_in.at[k, me], tp_s.at[k, p], tp_r.at[k, me], at(p)).wait_send()
+
+    peers(left)
 
     @pl.when(in_owner)
     def _():
-        each(quads, lambda d: copy(in_quad.at[member], in_quad.at[member], iq_s.at[d],
-                                   iq_r.at[member], over(quad_peer(d))).wait_send())
-        each(stacks, lambda d: copy(in_stack.at[layer], in_stack.at[layer], iz_s.at[d],
-                                    iz_r.at[layer], over(stack_peer(d))).wait_send())
-        each(NCTX, lambda d: copy(in_sums.at[in_index], in_sums.at[in_index], is_s.at[d],
-                                  is_r.at[in_index], at(other(d))).wait_send())
-
-    @pl.when(tap_owner)
-    def _():
-        each(NCTX, lambda d: copy(tap_sums.at[tap_index], tap_sums.at[tap_index], ts_s.at[d],
-                                  ts_r.at[tap_index], at(other(d))).wait_send())
+        each(chans, lambda d: copy(in_row.at[ch], in_row.at[ch], iq_s.at[d], iq_r.at[ch],
+                                   over(chan_peer(d))).wait_send())
+        peers(lambda p: copy(in_sums.at[in_index], in_sums.at[in_index], is_s.at[p],
+                             is_r.at[in_index], at(p)).wait_send())
 
 
 def hand_on(*refs):
@@ -613,8 +568,6 @@
 
 def per_device(consts, chans, query_proj, key_proj, value_proj, out_cotangent, short_taps,
                filter_in, filter_out, decay_rate, skip_gain):
-    quads = math.gcd(chans, 4)
-    stacks = chans // quads
     block = jax.ShapeDtypeStruct((256, POS), bf16)
     dma = pltpu.SemaphoreType.DMA
     V = pltpu.VMEM
@@ -628,7 +581,7 @@
               jax.ShapeDtypeStruct((1, OWN), f32))
     hbm = pl.BlockSpec(memory_space=pl.ANY)
     outs = pl.pallas_call(
-        functools.partial(kernel, quads, stacks),
+        functools.partial(kernel, chans),
         out_shape=shapes,
         in_specs=[hbm] * LOADS,
         out_specs=[hbm] * 8,
@@ -642,20 +595,18 @@
             V((2 * FH, SEQ), bf16), V((512, 128), f32),
             V((512, 128), f32), V((512, 128), f32),
             V((OWN * K1, 256), f32), V((OWN * K1, 256), f32), V((OWN * K1, 256), f32),
-            V((NCTX, 32, 256), bf16), V((NCTX, 32, 256), bf16),
-            V((NCTX, 16, 256), bf16), V((256, 256), bf16),
-            V((NCTX, 16, 256), bf16), V((256, 256), bf16),
+            V((NCTX, 16, 256), bf16), V((NCTX, 16, 256), bf16),
+            V((NCTX, 16, 256), bf16), V((NCTX, 16, 256), bf16),
+            V((NCTX, 16, 256), bf16), V((NCTX, 16, 256), bf16),
+            V((NCTX, 16, 256), bf16), V((NCTX, 16, 256), bf16),
             V((3 * OWN, SEQ), bf16), V((2 * FH, SEQ), bf16),
-            V((21, 256, 256), bf16), V((6, 8, 128), f32), V((NCTX, 8, 128), f32),
-            V((6, 8, 128), f32),
-            V((3, 8, 128), f32), V((NCTX, 8, 128), f32),
-            V((quads, 8, 128), f32), V((stacks, 8, 128), f32),
+            V((21, 256, 256), bf16), V((2, 16, 256), bf16), V((2, NCTX, 16, 256), bf16),
+            V((3, 8, 128), f32), V((NCTX, 8, 128), f32), V((chans, 8, 128), f32),
             V((3, 8, 128), f32), V((48, 128), f32),
-            dma((2,)), dma((2,)), dma((NCTX,)), dma((NCTX,)),
+            dma((2,)), dma((2,)), dma((NCTX,)), dma((NCTX,)), dma((NCTX,)), dma((NCTX,)),
             dma((NCTX,)), dma((NCTX,)), dma((NCTX,)), dma((NCTX,)),
-            dma((6,)), dma((NCTX,)), dma((NCTX,)), dma((6,)),
-            dma((3,)), dma((NCTX,)), dma((quads,)), dma((quads,)),
-            dma((stacks,)), dma((stacks,)), dma((NCTX,)), dma((3,)),
+            dma((2, NCTX)), dma((2, NCTX)), dma((3,)), dma((NCTX,)),
+            dma((chans,)), dma((chans,)), dma((NCTX,)), dma((3,)),
         ],
         compiler_params=pltpu.CompilerParams(
             collective_id=0, has_side_effects=True, vmem_limit_bytes=56 * 1024 * 1024),

time: 55.4 us -> 53 us (0.957)
  Pallas kernels: 54.6 us -> 52.1 us
    pallas_call x1, Pallas kernels: 52.7 us -> 50.2 us  [per_device(): pl.pallas_call(functools.partial(kernel, chans), out_shape=shapes, in_spe...]
where the time goes in v3:
time: 53 us; the launch traced here: 52.9 us
  Pallas kernels  52.1 us (98%)
  between operations  0.8 us (2%)
    pallas_call x1, Pallas kernels, per_device(): pl.pallas_call(functools.partial(kernel, chans), out_shape=shapes, in_spe...  50.2 us
    pallas_call x1, Pallas kernels, per_device(): pl.pallas_call(hand_on, out_shape=shapes, in_specs=[hbm] * 8, out_specs=[...  1.9 us

profile of v3, /device:TPU:2, one launch (start us, length us, event | category | flops | bytes accessed | tf_op | source)
XLA Modules:
  0.0 52.9 jit_solution(16345032825180114639)
XLA Ops:
  0.6 50.2 %shard_map.242 = (bf16[256,256]{1,0:T(8,128)(2,1)}, bf16[256,256]{1,0:T(8,128)(2,1)}, bf16[256,256]{1,0:T(8,128)(2,1)}, bf16[256,256]{1,0:T(8,128)(2,1)}, f32[3,...) custom-call(bf16[256,256]{1,0:T(8,128)(2,1)} %refs_0_.1, bf16[256,256]{1,0:T(8,128)(2,1)} %refs_1_.1, ...), custom_call_target="tpu_custom_call" | custom-call | tf_op jit(solution)/shard_map/pallas_call | solution.py:583
  50.8 1.9 %shard_map.243 = (bf16[256,256]{1,0:T(8,128)(2,1)}, bf16[256,256]{1,0:T(8,128)(2,1)}, bf16[256,256]{1,0:T(8,128)(2,1)}, bf16[256,256]{1,0:T(8,128)(2,1)}, f32[3,...) custom-call(bf16[256,256]{1,0:T(8,128)(2,1)} %get-tuple-element.24.refs_0_, ...), custom_call_target="tpu_custom_call" | custom-call | tf_op jit(solution)/shard_map/pallas_call | solution.py:614

commit v4 on v3

--- a/solution.py
+++ b/solution.py
@@ -130,6 +130,10 @@
      tp_s, tp_r, ip_s, ip_r, iq_s, iq_r, is_s, is_r) = refs
     me = lax.axis_index("ctx")
     ch = lax.axis_index("chan")
+    quads = math.gcd(chans, 4)
+    stacks = chans // quads
+    chan_steps = sorted(((dz, dw) for dz in range(stacks) for dw in range(quads) if dz + dw > 0),
+                        key=lambda s: (-min(s[0], stacks - s[0]) - s[1] // 2, s))
 
     def at(ctx_index):
         return {"ctx": ctx_index, "chan": ch}
@@ -153,8 +157,9 @@
         for dx, dy in STEPS:
             body(lax.rem(me // YS + dx, NCTX // YS) * YS + lax.rem(me % YS + dy, YS))
 
-    def chan_peer(d):
-        return lax.rem(ch + d, chans)
+    def chan_peers(body):
+        for n, (dz, dw) in enumerate(chan_steps):
+            body(n, lax.rem(ch // quads + dz, stacks) * quads + (ch % quads ^ dw))
 
     in_owner = jnp.logical_and(lax.rem(me, 2) == 1, me < 6)
     in_index = jnp.minimum(me // 2, 2)
@@ -168,7 +173,7 @@
 
     @pl.when(in_owner)
     def _():
-        each(chans, lambda d: greet(over(chan_peer(d))))
+        chan_peers(lambda n, p: greet(over(p)))
 
     def load(k):
         return pltpu.make_async_copy(sources[k], held[k], load_s.at[k])
@@ -454,17 +459,17 @@
         for p in range(1, NCTX):
             t = t + in_parts[p]
         in_row[ch] = t
-        each(chans, lambda d: copy(in_row.at[ch], in_row.at[ch], iq_s.at[d], iq_r.at[ch],
-                                   over(chan_peer(d))).start())
+        chan_peers(lambda n, p: copy(in_row.at[ch], in_row.at[ch], iq_s.at[n], iq_r.at[ch],
+                                     over(p)).start())
 
     load(17).wait()
     load(18).wait()
     wait_all(back_out, back_in, back_s, back_r)
     each(CHUNKS, back_part, 0)
+    tap_sum(1, (1, 2))
     heads_out[...] = mm(head_sel[...], ahead[...], 1, 1).astype(bf16)
     head_copy = copy(heads_out, heads_in, halo_s.at[1], halo_r.at[1], at(other(NCTX - 1)))
     head_copy.start()
-    tap_sum(1, (1, 2))
 
     head_copy.wait_recv()
     before_end = jnp.where(me < NCTX - 1, 1.0, 0.0)
@@ -497,10 +502,8 @@
 
     @pl.when(in_owner)
     def _():
-        def one(d):
-            p = chan_peer(d)
-            copy(in_row.at[p], in_row.at[p], iq_s.at[d], iq_r.at[p], over(p)).wait_recv()
-        each(chans, one)
+        chan_peers(lambda n, p: copy(in_row.at[p], in_row.at[p], iq_s.at[n], iq_r.at[p],
+                                     over(p)).wait_recv())
         t = in_row[0]
         for p in range(1, chans):
             t = t + in_row[p]
@@ -547,8 +550,8 @@
 
     @pl.when(in_owner)
     def _():
-        each(chans, lambda d: copy(in_row.at[ch], in_row.at[ch], iq_s.at[d], iq_r.at[ch],
-                                   over(chan_peer(d))).wait_send())
+        chan_peers(lambda n, p: copy(in_row.at[ch], in_row.at[ch], iq_s.at[n], iq_r.at[ch],
+                                     over(p)).wait_send())
         peers(lambda p: copy(in_sums.at[in_index], in_sums.at[in_index], is_s.at[p],
                              is_r.at[in_index], at(p)).wait_send())
 

time: 53 us -> 54.8 us (1.034)
  Pallas kernels: 52.1 us -> 53.8 us
    pallas_call x1, Pallas kernels: 50.2 us -> 51.9 us  [per_device(): pl.pallas_call(functools.partial(kernel, chans), out_shape=shapes, in_spe...]
where the time goes in v4:
time: 54.8 us; the launch traced here: 54.6 us
  Pallas kernels  53.8 us (98%)
  between operations  0.8 us (1%)
    pallas_call x1, Pallas kernels, per_device(): pl.pallas_call(functools.partial(kernel, chans), out_shape=shapes, in_spe...  51.9 us
    pallas_call x1, Pallas kernels, per_device(): pl.pallas_call(hand_on, out_shape=shapes, in_specs=[hbm] * 8, out_specs=[...  1.9 us

profile of v4, /device:TPU:2, one launch (start us, length us, event | category | flops | bytes accessed | tf_op | source)
XLA Modules:
  0.0 54.6 jit_solution(6851513449302832864)
XLA Ops:
  0.6 51.9 %shard_map.242 = (bf16[256,256]{1,0:T(8,128)(2,1)}, bf16[256,256]{1,0:T(8,128)(2,1)}, bf16[256,256]{1,0:T(8,128)(2,1)}, bf16[256,256]{1,0:T(8,128)(2,1)}, f32[3,...) custom-call(bf16[256,256]{1,0:T(8,128)(2,1)} %refs_0_.1, bf16[256,256]{1,0:T(8,128)(2,1)} %refs_1_.1, ...), custom_call_target="tpu_custom_call" | custom-call | tf_op jit(solution)/shard_map/pallas_call | solution.py:586
  52.5 1.9 %shard_map.243 = (bf16[256,256]{1,0:T(8,128)(2,1)}, bf16[256,256]{1,0:T(8,128)(2,1)}, bf16[256,256]{1,0:T(8,128)(2,1)}, bf16[256,256]{1,0:T(8,128)(2,1)}, f32[3,...) custom-call(bf16[256,256]{1,0:T(8,128)(2,1)} %get-tuple-element.24.refs_0_, ...), custom_call_target="tpu_custom_call" | custom-call | tf_op jit(solution)/shard_map/pallas_call | solution.py:617

commit v5 on v4

--- a/solution.py
+++ b/solution.py
@@ -363,9 +363,6 @@
     wait_all(u_out, u_in, u_s, u_r)
     unfold(u_in, sig_u)
     forward(sig_u, spec_u, True)
-    backward(spec_u, spec_h, False, sig_u)
-    fold(sig_u, u_in, conv_out)
-    scatter(conv_out, conv_in, conv_s, conv_r)
     wait_all(g_out, g_in, g_s, g_r)
     unfold(g_in, sig)
     forward(sig, spec_g, True)
@@ -401,6 +398,9 @@
                 go(copy(in_tiles.at[k], in_parts.at[me], ip_s.at[k], ip_r.at[me], at(2 * k + 1)))
 
     deal(lambda c: c.start())
+    backward(spec_u, spec_h, False, sig_u)
+    fold(sig_u, u_in, conv_out)
+    scatter(conv_out, conv_in, conv_s, conv_r)
     backward(spec_g, spec_h, True, sig)
     fold(sig, g_in, back_out)
     scatter(back_out, back_in, back_s, back_r)

time: 54.8 us -> 56.5 us (1.031)
  Pallas kernels: 53.8 us -> 55.6 us
    pallas_call x1, Pallas kernels: 51.9 us -> 53.7 us  [per_device(): pl.pallas_call(functools.partial(kernel, chans), out_shape=shapes, in_spe...]
where the time goes in v5:
time: 56.5 us; the launch traced here: 56.4 us
  Pallas kernels  55.6 us (98%)
  between operations  0.8 us (1%)
    pallas_call x1, Pallas kernels, per_device(): pl.pallas_call(functools.partial(kernel, chans), out_shape=shapes, in_spe...  53.7 us
    pallas_call x1, Pallas kernels, per_device(): pl.pallas_call(hand_on, out_shape=shapes, in_specs=[hbm] * 8, out_specs=[...  1.9 us

profile of v5, /device:TPU:2, one launch (start us, length us, event | category | flops | bytes accessed | tf_op | source)
XLA Modules:
  0.0 56.4 jit_solution(1613494160658113578)
XLA Ops:
  0.6 53.7 %shard_map.242 = (bf16[256,256]{1,0:T(8,128)(2,1)}, bf16[256,256]{1,0:T(8,128)(2,1)}, bf16[256,256]{1,0:T(8,128)(2,1)}, bf16[256,256]{1,0:T(8,128)(2,1)}, f32[3,...) custom-call(bf16[256,256]{1,0:T(8,128)(2,1)} %refs_0_.1, bf16[256,256]{1,0:T(8,128)(2,1)} %refs_1_.1, ...), custom_call_target="tpu_custom_call" | custom-call | tf_op jit(solution)/shard_map/pallas_call | solution.py:586
  54.3 1.9 %shard_map.243 = (bf16[256,256]{1,0:T(8,128)(2,1)}, bf16[256,256]{1,0:T(8,128)(2,1)}, bf16[256,256]{1,0:T(8,128)(2,1)}, bf16[256,256]{1,0:T(8,128)(2,1)}, f32[3,...) custom-call(bf16[256,256]{1,0:T(8,128)(2,1)} %get-tuple-element.24.refs_0_, ...), custom_call_target="tpu_custom_call" | custom-call | tf_op jit(solution)/shard_map/pallas_call | solution.py:617
